TPU v7x, 32 devices: a whole 2x2x4 slice. The times are simulated.
32 devices in a mesh: row: 4 (over y, core), col: 8 (over z, x).
Axes of the slice: x: 2, y: 2, z: 4, core: 2. Of those that a mesh axis runs over, the one named last changes fastest.
Arguments:
- layer_input: bfloat16 [1024, 12288], P('col', 'row'), may hold values from -6 to 6
- out_grad: bfloat16 [1024, 12288], P('col', 'row'), may hold values from -6 to 6
- preact: bfloat16 [1024, 16384], P('row', 'col'), may hold values from -6 to 6
- weight_in: bfloat16 [12288, 16384], P('row', 'col'), may hold values from -0.0546875 to 0.0546875
- weight_out: bfloat16 [16384, 12288], P('col', 'row'), may hold values from -0.046875 to 0.046875
Outputs:
- input_grad: bfloat16 [1024, 12288], P('col', 'row')
- weight_in_grad: float32 [12288, 16384], P('row', 'col')
- weight_out_grad: float32 [16384, 12288], P('col', 'row')
All inputs are finite; a program needn't handle non-finite values.
Results may differ from a plain program's by a relative error of at most 0.019.
Values may be sent and summed in bfloat16 or wider, within the bound.
A program may use at most 192 MiB of HBM per device.

v0:
```python
import math

import jax
import jax.numpy as jnp
from jax import lax
from jax.sharding import PartitionSpec as P


def gelu_parts(h):
    c = math.sqrt(2.0 / math.pi)
    t = jnp.tanh(c * (h + 0.044715 * h * h * h))
    value = 0.5 * h * (1.0 + t)
    slope = 0.5 * (1.0 + t) + 0.5 * h * (1.0 - t * t) * c * (1.0 + 3.0 * 0.044715 * h * h)
    return (value, slope)


def token_contract(left, right):
    return lax.dot_general(
        left, right, (((0,), (0,)), ((), ())), preferred_element_type=jnp.float32
    )


def width_contract(left, right):
    return lax.dot_general(
        left, right, (((1,), (1,)), ((), ())), preferred_element_type=jnp.float32
    )


def local(layer_input, out_grad, preact, weight_in, weight_out):
    input_panel, outgrad_panel = (
        lax.all_gather(layer_input, "col", axis=0, tiled=True),
        lax.all_gather(out_grad, "col", axis=0, tiled=True),
    )
    preact_full = lax.all_gather(preact, "row", axis=0, tiled=True)
    value, slope = gelu_parts(preact_full.astype(jnp.float32))
    activ_panel = value.astype(jnp.bfloat16)
    weight_out_grad = token_contract(activ_panel, outgrad_panel)
    tile_rows = preact.shape[0]
    part = outgrad_panel
    grad_act = lax.psum_scatter(
        width_contract(part, weight_out), "row", scatter_dimension=0, tiled=True
    )
    own_slope = lax.dynamic_slice_in_dim(slope, lax.axis_index("row") * tile_rows, tile_rows, 0)
    grad_pre = (grad_act * own_slope).astype(jnp.bfloat16)
    gradpre_panel = lax.all_gather(grad_pre, "row", axis=0, tiled=True)
    weight_in_grad = token_contract(input_panel, gradpre_panel)
    part = gradpre_panel
    input_grad = lax.psum_scatter(
        width_contract(part, weight_in).astype(jnp.bfloat16), "col", scatter_dimension=0, tiled=True
    )
    return (input_grad, weight_in_grad, weight_out_grad)


def solution(mesh):
    placed = (P("col", "row"), P("col", "row"), P("row", "col"), P("row", "col"), P("col", "row"))
    return jax.shard_map(
        local,
        mesh=mesh,
        in_specs=placed,
        out_specs=(P("col", "row"), P("row", "col"), P("col", "row")),
        check_vma=False,
    )
```

profile of v0, /device:TPU:0, one launch (start us, length us, event | category | flops | bytes accessed | tf_op | source)
XLA Modules:
  0.0 490.8 jit_solution(7773738456897246770)
XLA Ops:
  7.2 0.0 all-gather.5.cloned.1.call-start
  7.2 0.7 all-gather.5.cloned.1.call-update
  7.9 0.0 all-gather.7.cloned.1.call-start
  7.9 0.7 all-gather.7.cloned.1.call-update
  8.6 0.0 reduce-scatter.3.cloned.1.call-start
  8.7 103.2 %all-gather.5.cloned.1.call-done = bf16[1024,3072]{1,0:T(8,128)(2,1)} async-done(((bf16[128,3072]{1,0:T(8,128)(2,1)}), bf16[1024,3072]{1,0:T(8,128)(2,1)}) %all-gather.5.cloned.1.call-update) | async-done | bytes 6291472 | tf_op jit(solution)/shard_map/all_gather | solution.py:32
  111.9 18.9 %fusion.12 = f32[1024,2048]{1,0:T(8,128)} fusion(bf16[1024,3072]{1,0:T(8,128)(2,1)} %all-gather.5.cloned.1.call-done, bf16[2048,3072]{1,0:T(8,128)(2,1)} %param.9), kind=kOutput, calls=%fused_computation.21 | convolution fusion | flops 12884901888 | bytes 27262976 | tf_op jit(solution)/shard_map/dot_general | solution.py:24
  130.8 0.0 reduce-scatter.3.cloned.1.call-update
  130.8 0.0 all-gather.9.cloned.1.call-start
  130.9 15.3 %all-gather.7.cloned.1.call-done = bf16[1024,2048]{1,0:T(8,128)(2,1)} async-done(((bf16[256,2048]{1,0:T(8,128)(2,1)}), bf16[1024,2048]{1,0:T(8,128)(2,1)}) %all-gather.7.cloned.1.call-update) | async-done | bytes 4194320 | tf_op jit(solution)/shard_map/all_gather | solution.py:34
  146.2 6.6 %convert_element_type.12 = f32[1024,2048]{1,0:T(8,128)} convert(bf16[1024,2048]{1,0:T(8,128)(2,1)} %all-gather.7.cloned.1.call-done) | non-fusion elementwise | flops 2097152 | bytes 12582912 | tf_op jit(solution)/shard_map/convert_element_type | solution.py:35
  152.8 13.1 %fusion.1 = (f32[1024,2048]{1,0:T(8,128)}, f32[1024,2048]{1,0:T(8,128)}, f32[1024,2048]{1,0:T(8,128)}) fusion(bf16[1024,2048]{1,0:T(8,128)(2,1)S(1)} %copy-done), kind=kLoop, calls=%fused_computation.3 | loop fusion | flops 16777216 | bytes 29360128 | tf_op jit(solution)/shard_map/tanh | solution.py:11
  165.9 55.2 %reduce-scatter.3.cloned.1.call-done = f32[256,2048]{1,0:T(8,128)} async-done(((f32[1024,2048]{1,0:T(8,128)}), f32[256,2048]{1,0:T(8,128)}) %reduce-scatter.3.cloned.1.call-update) | async-done | bytes 2097168 | tf_op jit(solution)/shard_map/reduce_scatter | solution.py:40
  221.1 6.3 %fusion.7 = bf16[256,2048]{1,0:T(8,128)(2,1)} fusion(f32[256,2048]{1,0:T(8,128)} %reduce-scatter.3.cloned.1.call-done, f32[1024,2048]{1,0:T(8,128)} %get-tuple-element.7, s32[]{:T(128)S(6)} %select_n.3, f32[1024,2048]{1,0:T(8,128)} %get-tuple-element.8, f32[1024,2048]{1,0:T(8,128)} %convert_element_type.12, f32[1024,2048]{1,0:T(8,128)} %get-tuple-element.6), kind=kLoop, calls=%fused_computation.14 | loop fusion | flops 6291456 | bytes 11534340 | tf_op jit(solution)/shard_map/convert_element_type | solution.py:44
  227.4 0.0 all-gather.11.cloned.1.call-start
  227.4 0.5 all-gather.11.cloned.1.call-update
  228.0 0.2 reduce-scatter.5.cloned.1.call-start
  228.2 33.8 %all-gather.9.cloned.1.call-done = bf16[1024,2048]{1,0:T(8,128)(2,1)} async-done(((bf16[256,2048]{1,0:T(8,128)(2,1)}), bf16[1024,2048]{1,0:T(8,128)(2,1)}) %all-gather.9.cloned.1.call-update) | async-done | bytes 4194320 | tf_op jit(solution)/shard_map/all_gather | solution.py:45
  262.0 18.4 %convolution_convert_fusion = bf16[1024,3072]{1,0:T(8,128)(2,1)} fusion(bf16[1024,2048]{1,0:T(8,128)(2,1)} %all-gather.9.cloned.1.call-done, bf16[3072,2048]{1,0:T(8,128)(2,1)} %param.8), kind=kOutput, calls=%fused_computation.5 | convolution fusion | flops 12888047616 | bytes 23068672 | tf_op jit(solution)/shard_map/dot_general | solution.py:24
  280.5 25.3 %fusion.2 = f32[2048,3072]{1,0:T(8,128)} fusion(bf16[1024,3072]{1,0:T(8,128)(2,1)} %all-gather.5.cloned.1.call-done, bf16[1024,2048]{1,0:T(8,128)(2,1)} %all-gather.7.cloned.1.call-done), kind=kOutput, calls=%fused_computation.6 | convolution fusion | flops 12905873408 | bytes 35651584 | tf_op jit(solution)/shard_map/dot_general | solution.py:18
  305.8 57.5 %all-gather.11.cloned.1.call-done = bf16[1024,3072]{1,0:T(8,128)(2,1)} async-done(((bf16[128,3072]{1,0:T(8,128)(2,1)}), bf16[1024,3072]{1,0:T(8,128)(2,1)}) %all-gather.11.cloned.1.call-update) | async-done | bytes 6291472 | tf_op jit(solution)/shard_map/all_gather | solution.py:31
  363.4 20.0 %convolution_bitcast_fusion = f32[3072,2048]{0,1:T(8,128)} fusion(bf16[1024,2048]{1,0:T(8,128)(2,1)} %all-gather.9.cloned.1.call-done, bf16[1024,3072]{1,0:T(8,128)(2,1)} %all-gather.11.cloned.1.call-done), kind=kOutput, calls=%fused_computation | convolution fusion | flops 12884901888 | bytes 35651584 | tf_op jit(solution)/shard_map/dot_general | solution.py:18
  383.3 24.9 %copy.8 = f32[3072,2048]{1,0:T(8,128)} copy(f32[3072,2048]{0,1:T(8,128)} %convolution_bitcast_fusion) | data formatting | bytes 50331648
  408.2 75.8 %reduce-scatter.5.cloned.1.call-done = bf16[128,3072]{1,0:T(8,128)(2,1)} async-done(((bf16[1024,3072]{1,0:T(8,128)(2,1)}), bf16[128,3072]{1,0:T(8,128)(2,1)}) %reduce-scatter.5.cloned.1.call-update) | async-done | bytes 786448 | tf_op jit(solution)/shard_map/reduce_scatter | solution.py:48
  (4 shorter events, 0.0 us)
Async XLA Ops:
  7.2 104.8 %all-gather.5.cloned.1.call-start = ((), (), s32[]{:S(2)}) async-start(), calls=%async_computation.2 | async-start | bytes 7077888 | tf_op jit(solution)/shard_map/all_gather | solution.py:32
  7.9 138.3 %all-gather.7.cloned.1.call-start = ((), (), s32[]{:S(2)}) async-start(), calls=%async_computation.4 | async-start | bytes 5242880 | tf_op jit(solution)/shard_map/all_gather | solution.py:34
  8.6 212.5 %reduce-scatter.3.cloned.1.call-start = ((), (), s32[]{:S(2)}) async-start(), calls=%async_computation.3 | async-start | bytes 10485760 | tf_op jit(solution)/shard_map/reduce_scatter | solution.py:40
  130.8 131.2 %all-gather.9.cloned.1.call-start = ((), (), s32[]{:S(2)}) async-start(), calls=%async_computation.5 | async-start | bytes 5242880 | tf_op jit(solution)/shard_map/all_gather | solution.py:45
  146.2 6.6 %copy-start = (bf16[1024,2048]{1,0:T(8,128)(2,1)S(1)}, bf16[1024,2048]{1,0:T(8,128)(2,1)}, u32[]{:S(2)}) copy-start(bf16[1024,2048]{1,0:T(8,128)(2,1)} %all-gather.7.cloned.1.call-done) | copy-start | bytes 12582916
  227.4 136.0 %all-gather.11.cloned.1.call-start = ((), (), s32[]{:S(2)}) async-start(), calls=%async_computation.7 | async-start | bytes 7077888 | tf_op jit(solution)/shard_map/all_gather | solution.py:31
  228.0 256.0 %reduce-scatter.5.cloned.1.call-start = ((), (), s32[]{:S(2)}) async-start(), calls=%async_computation.6 | async-start | bytes 7077888 | tf_op jit(solution)/shard_map/reduce_scatter | solution.py:48
Sparse Core Ops, SparseCore 0:
  10.2 101.7 all-gather.4
  113.5 32.6 all-gather.6
  149.4 71.7 reduce-scatter.2
  227.5 34.4 all-gather.8
  264.3 99.0 all-gather.10
  367.8 116.1 reduce-scatter.4
where the time goes:
time: 491 us
  waiting for transfers between devices  343 us (70%)
  matrix products  82.6 us (17%)
  other arithmetic  26 us (5%)
  local copies, waits for them, and re-layouts  24.9 us (5%)
  between operations  14.1 us (3%)
    all_gather x1, waiting for transfers between devices, local(): lax.all_gather(out_grad, 'col', axis=0, tiled=True)  103 us
    reduce_scatter x1, waiting for transfers between devices, local(): lax.psum_scatter(width_contract(part, weight_in).astype(jnp.bfloat16), 'c...  75.8 us
    all_gather x1, waiting for transfers between devices, local(): lax.all_gather(layer_input, 'col', axis=0, tiled=True)  57.5 us
    reduce_scatter x1, waiting for transfers between devices, local(): lax.psum_scatter(width_contract(part, weight_out), 'row', scatter_dimensi...  55.2 us
    dot_general x2, matrix products, token_contract(): lax.dot_general(left, right, (((0,), (0,)), ((), ())), preferred_element_...  45.3 us
    dot_general x2, matrix products, width_contract(): lax.dot_general(left, right, (((1,), (1,)), ((), ())), preferred_element_...  37.3 us
    all_gather x1, waiting for transfers between devices, local(): gradpre_panel = lax.all_gather(grad_pre, 'row', axis=0, tiled=True)  33.8 us
    unnamed x3, local copies, waits for them, and re-layouts  24.9 us
  transfers between devices with their start and end apart: 6, of which 6 were waited for; matrix products, arithmetic and copies ran while one was open for 26% of the time, Pallas kernels for 0%

commit v1 on v0

v1 whole, which is shorter than its diff:
```python
import functools
import math

import jax
import jax.numpy as jnp
from jax import lax
from jax.experimental import pallas as pl
from jax.experimental.pallas import tpu as pltpu
from jax.sharding import PartitionSpec as P

MESH = pl.DeviceIdType.MESH
BF16 = jnp.bfloat16
F32 = jnp.float32


def gelu_parts(h):
    c = math.sqrt(2.0 / math.pi)
    t = jnp.tanh(c * (h + 0.044715 * h * h * h))
    value = 0.5 * h * (1.0 + t)
    slope = 0.5 * (1.0 + t) + 0.5 * h * (1.0 - t * t) * c * (1.0 + 3.0 * 0.044715 * h * h)
    return (value, slope)


def token_contract(left, right):
    return lax.dot_general(
        left, right, (((0,), (0,)), ((), ())), preferred_element_type=jnp.float32
    )


def width_contract(left, right):
    return lax.dot_general(
        left, right, (((1,), (1,)), ((), ())), preferred_element_type=jnp.float32
    )


class ColGather:
    def __init__(self, n, own, panel, sems):
        self.lines = n // 2
        me = lax.axis_index("col")
        self.z, self.x = me // 2, me % 2
        self.own, self.panel = own, panel
        self.rows = own.shape[0]
        self.local, self.up, self.down, self.across, self.from_line, self.from_mate = sems

    def block(self, z, x):
        return self.panel.at[pl.ds((z * 2 + x) * self.rows, self.rows)]

    def copy(self, src, z, send, recv, target):
        return pltpu.make_async_remote_copy(
            src_ref=src, dst_ref=self.block(z, self.x), send_sem=send.at[z], recv_sem=recv.at[z],
            device_id={"col": target}, device_id_type=MESH,
        )

    def up_copy(self, z, src):
        return self.copy(src, z, self.up, self.from_line, (self.z + 1) * 2 + self.x)

    def down_copy(self, z, src):
        return self.copy(src, z, self.down, self.from_line, (self.z - 1) * 2 + self.x)

    def across_copy(self, z, src):
        return self.copy(src, z, self.across, self.from_mate, self.z * 2 + 1 - self.x)

    def start(self):
        pltpu.make_async_copy(self.own, self.block(self.z, self.x), self.local.at[0]).start()

        @pl.when(self.z < self.lines - 1)
        def _():
            self.up_copy(self.z, self.own).start()

        @pl.when(self.z > 0)
        def _():
            self.down_copy(self.z, self.own).start()

        self.across_copy(self.z, self.own).start()

    def wait_line(self, z):
        block = self.block(z, self.x)
        self.copy(block, z, self.up, self.from_line, self.z * 2 + 1 - self.x).wait_recv()

    def wait_mate(self, z):
        block = self.block(z, 1 - self.x)
        pltpu.make_async_remote_copy(
            src_ref=block, dst_ref=block, send_sem=self.across.at[z], recv_sem=self.from_mate.at[z],
            device_id={"col": self.z * 2 + 1 - self.x}, device_id_type=MESH,
        ).wait_recv()

    def step(self, s):
        @pl.when(self.z >= s)
        def _():
            z = self.z - s
            self.wait_line(z)
            self.across_copy(z, self.block(z, self.x)).start()

            @pl.when(self.z < self.lines - 1)
            def _():
                self.up_copy(z, self.block(z, self.x)).start()

        @pl.when(self.z + s < self.lines)
        def _():
            z = self.z + s
            self.wait_line(z)
            self.across_copy(z, self.block(z, self.x)).start()

            @pl.when(self.z > 0)
            def _():
                self.down_copy(z, self.block(z, self.x)).start()

    def wait_own(self):
        pltpu.make_async_copy(self.own, self.block(self.z, self.x), self.local.at[0]).wait()

    def end(self):
        for s in range(self.lines):
            @pl.when(self.z >= s)
            def _():
                z = self.z - s
                self.across_copy(z, self.block(z, self.x)).wait_send()

                @pl.when(self.z < self.lines - 1)
                def _():
                    self.up_copy(z, self.block(z, self.x)).wait_send()

            @pl.when(self.z + s < self.lines)
            def _():
                z = self.z + s
                if s > 0:
                    self.across_copy(z, self.block(z, self.x)).wait_send()

                @pl.when(self.z > 0)
                def _():
                    self.down_copy(z, self.block(z, self.x)).wait_send()


class RowGather:
    def __init__(self, n, own, panel, sems):
        self.outer = n // 2
        me = lax.axis_index("row")
        self.o, self.c = me // 2, me % 2
        self.own, self.panel = own, panel
        self.rows = own.shape[0]
        self.local, self.far, self.across, self.from_far, self.from_mate = sems

    def block(self, o, c):
        return self.panel.at[pl.ds((o * 2 + c) * self.rows, self.rows)]

    def far_copy(self, o):
        return pltpu.make_async_remote_copy(
            src_ref=self.own, dst_ref=self.block(self.o, self.c), send_sem=self.far.at[o],
            recv_sem=self.from_far.at[self.o], device_id={"row": o * 2 + self.c}, device_id_type=MESH,
        )

    def across_copy(self, o, src):
        return pltpu.make_async_remote_copy(
            src_ref=src, dst_ref=self.block(o, self.c), send_sem=self.across.at[o],
            recv_sem=self.from_mate.at[o], device_id={"row": self.o * 2 + 1 - self.c}, device_id_type=MESH,
        )

    def start(self):
        for k in range(1, self.outer):
            self.far_copy((self.o + k) % self.outer).start()
        self.across_copy(self.o, self.own).start()
        pltpu.make_async_copy(self.own, self.block(self.o, self.c), self.local.at[0]).start()

    def forward(self):
        for k in range(1, self.outer):
            o = (self.o + self.outer - k) % self.outer
            block = self.block(o, self.c)
            pltpu.make_async_remote_copy(
                src_ref=block, dst_ref=block, send_sem=self.far.at[o], recv_sem=self.from_far.at[o],
                device_id={"row": o * 2 + self.c}, device_id_type=MESH,
            ).wait_recv()
            self.across_copy(o, block).start()

    def end(self):
        pltpu.make_async_copy(self.own, self.block(self.o, self.c), self.local.at[0]).wait()
        for k in range(1, self.outer):
            self.far_copy((self.o + k) % self.outer).wait_send()
        for k in range(self.outer):
            o = (self.o + k) % self.outer
            self.across_copy(o, self.block(o, self.c)).wait_send()
            block = self.block(o, 1 - self.c)
            pltpu.make_async_remote_copy(
                src_ref=block, dst_ref=block, send_sem=self.across.at[o], recv_sem=self.from_mate.at[o],
                device_id={"row": self.o * 2 + 1 - self.c}, device_id_type=MESH,
            ).wait_recv()


def col_sems(n):
    lines = n // 2
    return [pltpu.SemaphoreType.DMA((1,))] + [pltpu.SemaphoreType.DMA((lines,))] * 5


def row_sems(n):
    return [pltpu.SemaphoreType.DMA((1,))] + [pltpu.SemaphoreType.DMA((n // 2,))] * 4


def greet(rows, cols):
    barrier = pltpu.get_barrier_semaphore()
    me_r, me_c = lax.axis_index("row"), lax.axis_index("col")
    outer, lines = rows // 2, cols // 2
    o, c, z, x = me_r // 2, me_r % 2, me_c // 2, me_c % 2
    count = 0
    if rows:
        for k in range(1, outer):
            pl.semaphore_signal(
                barrier, inc=1, device_id={"row": ((o + k) % outer) * 2 + c}, device_id_type=MESH
            )
        pl.semaphore_signal(barrier, inc=1, device_id={"row": o * 2 + 1 - c}, device_id_type=MESH)
        count = outer
    pl.semaphore_signal(barrier, inc=1, device_id={"col": z * 2 + 1 - x}, device_id_type=MESH)

    @pl.when(z > 0)
    def _():
        pl.semaphore_signal(barrier, inc=1, device_id={"col": (z - 1) * 2 + x}, device_id_type=MESH)

    @pl.when(z < lines - 1)
    def _():
        pl.semaphore_signal(barrier, inc=1, device_id={"col": (z + 1) * 2 + x}, device_id_type=MESH)

    count = count + 1 + jnp.where(z > 0, 1, 0) + jnp.where(z < lines - 1, 1, 0)
    pl.semaphore_wait(barrier, count)


STRIP = 16
COLS = 256


def hidden_kernel(
    n_row, n_col,
    li_ref, og_ref, pre_ref, wo_ref,
    li_panel, og_panel, act_panel, gp_panel,
    wo, pair, part, pre, act, slope, first, second, outgoing, own_gp,
    load_sem, s1_send, s1_recv, s2_send, s2_recv, *sems,
):
    og = ColGather(n_col, og_ref, og_panel, sems[0:6])
    li = ColGather(n_col, li_ref, li_panel, sems[6:12])
    act_rows = RowGather(n_row, act, act_panel, sems[12:17])
    gp_rows = RowGather(n_row, own_gp, gp_panel, sems[17:22])
    lines, outer = n_col // 2, n_row // 2
    rows = pre_ref.shape[0]
    me = lax.axis_index("row")
    o, c = me // 2, me % 2

    greet(n_row, n_col)
    og.start()
    load_pre = pltpu.make_async_copy(pre_ref, pre, load_sem.at[0])
    load_pre.start()
    load_wo = pltpu.make_async_copy(wo_ref, wo, load_sem.at[1])
    load_wo.start()

    load_pre.wait()

    @pl.loop(0, rows // STRIP)
    def _(i):
        r = pl.ds(pl.multiple_of(i * STRIP, STRIP), STRIP)
        v, d = gelu_parts(pre[r, :].astype(F32))
        act[r, :] = v.astype(BF16)
        slope[r, :] = d

    act_rows.start()
    load_wo.wait()
    og.wait_own()

    def multiply(z):
        size = 2 * og.rows
        start = pl.multiple_of(z * size, size)
        og.wait_mate(z)
        fetch = pltpu.make_async_copy(og_panel.at[pl.ds(start, size)], pair, load_sem.at[2])
        fetch.start()
        fetch.wait()

        @pl.loop(0, wo.shape[0] // COLS)
        def _(j):
            k = pl.ds(pl.multiple_of(j * COLS, COLS), COLS)
            part[pl.ds(start, size), k] = width_contract(pair[...], wo[k, :]).astype(BF16)

    def multiply_step(s):
        if s == 0:
            multiply(og.z)
        else:
            pl.when(og.z >= s)(lambda: multiply(og.z - s))
            pl.when(og.z + s < lines)(lambda: multiply(og.z + s))

    for s in range(1, lines):
        og.step(s)
        if s == lines - 1:
            li.start()
        multiply_step(s - 1)
    act_rows.forward()
    multiply_step(lines - 1)

    def own_rows(q):
        return pl.ds(pl.multiple_of(q * rows, rows), rows)

    def first_copy(k):
        return pltpu.make_async_remote_copy(
            src_ref=part.at[own_rows(k * 2 + 1 - c)], dst_ref=first.at[k], send_sem=s1_send.at[k],
            recv_sem=s1_recv.at[k], device_id={"row": o * 2 + 1 - c}, device_id_type=MESH,
        )

    def second_copy(k):
        return pltpu.make_async_remote_copy(
            src_ref=outgoing.at[k], dst_ref=second.at[o], send_sem=s2_send.at[k],
            recv_sem=s2_recv.at[o], device_id={"row": k * 2 + c}, device_id_type=MESH,
        )

    order = [(o + k) % outer for k in range(1, outer)] + [o]
    for k in order:
        first_copy(k).start()
    for k in order[:-1]:
        first_copy(k).wait_recv()

        @pl.loop(0, rows // STRIP)
        def _(i):
            at = pl.multiple_of(i * STRIP, STRIP)
            mine = part[pl.ds(pl.multiple_of((k * 2 + c) * rows + at, STRIP), STRIP), :]
            r = pl.ds(at, STRIP)
            outgoing[k, r, :] = (mine.astype(F32) + first[k, r, :].astype(F32)).astype(BF16)

        second_copy(k).start()

    li.wait_own()
    steps = list(range(1, lines))
    early = steps[: max(1, len(steps) // 3)]
    for s in early:
        li.step(s)

    first_copy(o).wait_recv()
    for k in order[:-1]:
        pltpu.make_async_remote_copy(
            src_ref=outgoing.at[k], dst_ref=second.at[k], send_sem=s2_send.at[k],
            recv_sem=s2_recv.at[k], device_id={"row": k * 2 + c}, device_id_type=MESH,
        ).wait_recv()

    @pl.loop(0, rows // STRIP)
    def _(i):
        at = pl.multiple_of(i * STRIP, STRIP)
        r = pl.ds(at, STRIP)
        total = part[pl.ds(pl.multiple_of(me * rows + at, STRIP), STRIP), :].astype(F32)
        total = total + first[o, r, :].astype(F32)
        for k in order[:-1]:
            total = total + second[k, r, :].astype(F32)
        own_gp[r, :] = (total * slope[r, :]).astype(BF16)

    gp_rows.start()
    for s in steps[len(early):]:
        li.step(s)
    gp_rows.forward()

    for k in order:
        first_copy(k).wait_send()
    for k in order[:-1]:
        second_copy(k).wait_send()
    act_rows.end()
    gp_rows.end()
    og.end()
    for s in range(lines):
        if s == 0:
            li.wait_mate(li.z)
        else:
            pl.when(li.z >= s)(lambda: li.wait_mate(li.z - s))
            pl.when(li.z + s < lines)(lambda: li.wait_mate(li.z + s))
    li.end()


def hidden(n_row, n_col, layer_input, out_grad, preact, weight_out):
    t, d = layer_input.shape
    rows, f = preact.shape
    tokens = t * n_col
    outer = n_row // 2
    any_spec = pl.BlockSpec(memory_space=pl.ANY)
    return pl.pallas_call(
        functools.partial(hidden_kernel, n_row, n_col),
        out_shape=[
            jax.ShapeDtypeStruct((tokens, d), BF16),
            jax.ShapeDtypeStruct((tokens, d), BF16),
            jax.ShapeDtypeStruct((tokens, f), BF16),
            jax.ShapeDtypeStruct((tokens, f), BF16),
        ],
        in_specs=[any_spec] * 4,
        out_specs=[any_spec] * 4,
        scratch_shapes=[
            pltpu.VMEM((f, d), BF16),
            pltpu.VMEM((2 * t, d), BF16),
            pltpu.VMEM((tokens, f), BF16),
            pltpu.VMEM((rows, f), BF16),
            pltpu.VMEM((rows, f), BF16),
            pltpu.VMEM((rows, f), F32),
            pltpu.VMEM((outer, rows, f), BF16),
            pltpu.VMEM((outer, rows, f), BF16),
            pltpu.VMEM((outer, rows, f), BF16),
            pltpu.VMEM((rows, f), BF16),
            pltpu.SemaphoreType.DMA((3,)),
        ]
        + [pltpu.SemaphoreType.DMA((outer,))] * 4
        + col_sems(n_col) * 2
        + row_sems(n_row) * 2,
        compiler_params=pltpu.CompilerParams(
            collective_id=0, has_side_effects=True, vmem_limit_bytes=50 * 2**20
        ),
        cost_estimate=pl.CostEstimate(
            flops=2 * tokens * d * f, bytes_accessed=2 * (f * d + 4 * tokens * (d + f)), transcendentals=rows * f
        ),
        name="hidden",
    )(layer_input, out_grad, preact, weight_out)


def local(n_row, n_col, layer_input, out_grad, preact, weight_in, weight_out):
    li_panel, og_panel, act_panel, gp_panel = hidden(
        n_row, n_col, layer_input, out_grad, preact, weight_out
    )
    input_grad = lax.psum_scatter(
        width_contract(gp_panel, weight_in).astype(BF16), "col", scatter_dimension=0, tiled=True
    )
    weight_out_grad = token_contract(act_panel, og_panel)
    weight_in_grad = token_contract(li_panel, gp_panel)
    return (input_grad, weight_in_grad, weight_out_grad)


def solution(mesh):
    placed = (P("col", "row"), P("col", "row"), P("row", "col"), P("row", "col"), P("col", "row"))
    return jax.shard_map(
        functools.partial(local, mesh.shape["row"], mesh.shape["col"]),
        mesh=mesh,
        in_specs=placed,
        out_specs=(P("col", "row"), P("row", "col"), P("col", "row")),
        check_vma=False,
    )
```

time: 491 us -> 298 us (0.61)
  waiting for transfers between devices: 343 us -> 79.7 us
  Pallas kernels: 0 us -> 145 us
  matrix products: 82.6 us -> 55.6 us
  other arithmetic: 26 us -> 0.01 us
  local copies, waits for them, and re-layouts: 24.9 us -> 3.5 us
    all_gather x4 -> x0, waiting for transfers between devices: 210 us -> none  [the longest x1 103 us: local(): lax.all_gather(out_grad, 'col', axis=0, tiled=True)]
    pallas_call x0 -> x1, Pallas kernels: none -> 145 us  [hidden(): pl.pallas_call(functools.partial(hidden_kernel, n_row, n_col), out_shape=...]
    reduce_scatter x2 -> x1, waiting for transfers between devices: 131 us -> 79.7 us  [local(): lax.psum_scatter(width_contract(gp_panel, weight_in).astype(BF16), 'col',...]
    unnamed x3 -> x12, local copies, waits for them, and re-layouts: 24.9 us -> 3.5 us
    dot_general x2 -> x1, matrix products: 37.3 us -> 18.5 us  [width_contract(): lax.dot_general(left, right, (((1,), (1,)), ((), ())), preferred_element_...]
    tanh x1 -> x0, other arithmetic: 13.1 us -> none  [gelu_parts(): t = jnp.tanh(c * (h + 0.044715 * h * h * h))]
    convert_element_type x2 -> x0, other arithmetic: 12.9 us -> none  [the longest x1 6.63 us: local(): value, slope = gelu_parts(preact_full.astype(jnp.float32))]
    dot_general x2, matrix products: 45.3 us -> 37.1 us  [token_contract(): lax.dot_general(left, right, (((0,), (0,)), ((), ())), preferred_element_...]
  transfers between devices with their start and end apart: 6 -> 1, of which waited for: 6 -> 1; matrix products, arithmetic and copies ran while one was open for 26% -> 12% of each run, Pallas kernels for 0% -> 0%
where the time goes in v1:
time: 298 us
  Pallas kernels  145 us (49%)
  waiting for transfers between devices  79.7 us (27%)
  matrix products  55.6 us (19%)
  between operations  14.1 us (5%)
  local copies, waits for them, and re-layouts  3.5 us (1%)
    pallas_call x1, Pallas kernels, hidden(): pl.pallas_call(functools.partial(hidden_kernel, n_row, n_col), out_shape=...  145 us
    reduce_scatter x1, waiting for transfers between devices, local(): lax.psum_scatter(width_contract(gp_panel, weight_in).astype(BF16), 'col',...  79.7 us
    dot_general x2, matrix products, token_contract(): lax.dot_general(left, right, (((0,), (0,)), ((), ())), preferred_element_...  37.1 us
    dot_general x1, matrix products, width_contract(): lax.dot_general(left, right, (((1,), (1,)), ((), ())), preferred_element_...  18.5 us
  transfers between devices with their start and end apart: 1, of which 1 were waited for; matrix products, arithmetic and copies ran while one was open for 12% of the time, Pallas kernels for 0%

profile of v1, /device:TPU:0, one launch (start us, length us, event | category | flops | bytes accessed | tf_op | source)
XLA Modules:
  0.0 297.7 jit_solution(3437609023598293582)
XLA Ops:
  7.2 0.0 reduce-scatter.2.cloned.1.call-start
  7.2 0.0 copy-start
  7.2 1.2 copy-done
  8.4 0.0 copy-start.1
  8.4 1.1 copy-done.1
  9.6 0.0 copy-start.2
  9.6 1.1 copy-done.2
  10.7 144.8 %hidden.1 = (bf16[1024,3072]{1,0:T(8,128)(2,1)}, bf16[1024,3072]{1,0:T(8,128)(2,1)}, bf16[1024,2048]{1,0:T(8,128)(2,1)}, bf16[1024,2048]{1,0:T(8,128)(2,1)}) custom-call(bf16[128,3072]{1,0:T(8,128)(2,1)S(1)} %copy-done.1, bf16[128,3072]{1,0:T(8,128)(2,1)S(1)} %copy-done.2, bf16[256,2048]{1,0:T(8,128)(2,1)S(1)} %copy-done, bf16[2048,3072]{1,0:T(8,128)(2,1)} %wo_ref.1), custom_call_target="tpu_custom_call" | custom-call | flops 12884901888 | bytes 54525952 | tf_op jit(solution)/shard_map/hidden/pallas_call | solution.py:371
  155.5 18.5 %convolution_convert_fusion = bf16[1024,3072]{1,0:T(8,128)(2,1)} fusion(bf16[1024,2048]{1,0:T(8,128)(2,1)} %get-tuple-element.7, bf16[3072,2048]{1,0:T(8,128)(2,1)} %param.8), kind=kOutput, calls=%fused_computation | convolution fusion | flops 12888047616 | bytes 23068672 | tf_op jit(solution)/shard_map/dot_general | solution.py:31
  174.0 0.0 slice-start
  174.0 0.0 reduce-scatter.2.cloned.1.call-update
  174.0 0.0 slice-start.1
  174.1 0.0 copy-start.3
  174.1 20.1 %fusion = f32[3072,2048]{1,0:T(8,128)} fusion(bf16[1024,3072]{1,0:T(8,128)(2,1)} %get-tuple-element.8, bf16[1024,2048]{1,0:T(8,128)(2,1)} %get-tuple-element.7), kind=kOutput, calls=%fused_computation.1 | convolution fusion | flops 12884901888 | bytes 35651584 | tf_op jit(solution)/shard_map/dot_general | solution.py:25
  194.2 0.0 slice-done
  194.2 0.0 slice-done.1
  194.2 0.0 copy-done.3
  194.2 17.0 %fusion.1 = f32[2048,3072]{1,0:T(8,128)} fusion(bf16[1024,2048]{1,0:T(8,128)(2,1)S(1)} %copy-done.3, bf16[1024,3072]{1,0:T(8,128)(2,1)S(1)} %bitcast.7), kind=kOutput, calls=%fused_computation.2 | convolution fusion | flops 12884901888 | bytes 35651584 | tf_op jit(solution)/shard_map/dot_general | solution.py:25
  211.2 79.7 %reduce-scatter.2.cloned.1.call-done = bf16[128,3072]{1,0:T(8,128)(2,1)} async-done(((bf16[1024,3072]{1,0:T(8,128)(2,1)}), bf16[128,3072]{1,0:T(8,128)(2,1)}) %reduce-scatter.2.cloned.1.call-update) | async-done | bytes 786448 | tf_op jit(solution)/shard_map/reduce_scatter | solution.py:411
  (1 shorter events, 0.0 us)
Async XLA Ops:
  7.2 283.7 %reduce-scatter.2.cloned.1.call-start = ((), (), s32[]{:S(2)}) async-start(), calls=%async_computation.1 | async-start | bytes 7077888 | tf_op jit(solution)/shard_map/reduce_scatter | solution.py:411
  7.2 1.2 copy-start
  8.4 1.1 copy-start.1
  9.6 1.1 copy-start.2
  174.0 20.2 %slice-start = ((s8[6291456]{0:T(1024)(128)(4,1)}), s8[2097152]{0:T(1024)(128)(4,1)S(1)}, s32[]{:S(2)}) async-start(s8[6291456]{0:T(1024)(128)(4,1)} %bitcast.6), calls=%async_computation.2 | async-start | bytes 4194304
  174.0 20.2 %slice-start.1 = ((s8[6291456]{0:T(1024)(128)(4,1)}), s8[4194304]{0:T(1024)(128)(4,1)S(1)}, s32[]{:S(2)}) async-start(s8[6291456]{0:T(1024)(128)(4,1)} %bitcast.6), calls=%async_computation.3 | async-start | bytes 8388608
  174.1 20.1 %copy-start.3 = (bf16[1024,2048]{1,0:T(8,128)(2,1)S(1)}, bf16[1024,2048]{1,0:T(8,128)(2,1)}, u32[]{:S(2)}) copy-start(bf16[1024,2048]{1,0:T(8,128)(2,1)} %get-tuple-element.9) | copy-start | bytes 12582916
Sparse Core Ops, SparseCore 0:
  174.2 116.6 reduce-scatter.1

commit v2 on v1

--- a/solution.py
+++ b/solution.py
@@ -3,6 +3,7 @@
 
 import jax
 import jax.numpy as jnp
+import numpy as np
 from jax import lax
 from jax.experimental import pallas as pl
 from jax.experimental.pallas import tpu as pltpu
@@ -11,6 +12,7 @@
 MESH = pl.DeviceIdType.MESH
 BF16 = jnp.bfloat16
 F32 = jnp.float32
+PIECES = 2
 
 
 def gelu_parts(h):
@@ -40,94 +42,90 @@
         self.z, self.x = me // 2, me % 2
         self.own, self.panel = own, panel
         self.rows = own.shape[0]
+        self.size = self.rows // PIECES
         self.local, self.up, self.down, self.across, self.from_line, self.from_mate = sems
 
-    def block(self, z, x):
-        return self.panel.at[pl.ds((z * 2 + x) * self.rows, self.rows)]
-
-    def copy(self, src, z, send, recv, target):
+    def block(self, z, x, h):
+        return self.panel.at[pl.ds((z * 2 + x) * self.rows + h * self.size, self.size)]
+
+    def source(self, z, h, mine):
+        return self.own.at[pl.ds(h * self.size, self.size)] if mine else self.block(z, self.x, h)
+
+    def copy(self, src, z, h, send, recv, target):
         return pltpu.make_async_remote_copy(
-            src_ref=src, dst_ref=self.block(z, self.x), send_sem=send.at[z], recv_sem=recv.at[z],
-            device_id={"col": target}, device_id_type=MESH,
-        )
-
-    def up_copy(self, z, src):
-        return self.copy(src, z, self.up, self.from_line, (self.z + 1) * 2 + self.x)
-
-    def down_copy(self, z, src):
-        return self.copy(src, z, self.down, self.from_line, (self.z - 1) * 2 + self.x)
-
-    def across_copy(self, z, src):
-        return self.copy(src, z, self.across, self.from_mate, self.z * 2 + 1 - self.x)
+            src_ref=src, dst_ref=self.block(z, self.x, h), send_sem=send.at[z * PIECES + h],
+            recv_sem=recv.at[z * PIECES + h], device_id={"col": target}, device_id_type=MESH,
+        )
+
+    def up_copy(self, z, h, mine=False):
+        return self.copy(self.source(z, h, mine), z, h, self.up, self.from_line, (self.z + 1) * 2 + self.x)
+
+    def down_copy(self, z, h, mine=False):
+        return self.copy(self.source(z, h, mine), z, h, self.down, self.from_line, (self.z - 1) * 2 + self.x)
+
+    def across_copy(self, z, h, mine=False):
+        return self.copy(self.source(z, h, mine), z, h, self.across, self.from_mate, self.z * 2 + 1 - self.x)
+
+    def own_copy(self):
+        return pltpu.make_async_copy(
+            self.own, self.panel.at[pl.ds((self.z * 2 + self.x) * self.rows, self.rows)], self.local.at[0]
+        )
 
     def start(self):
-        pltpu.make_async_copy(self.own, self.block(self.z, self.x), self.local.at[0]).start()
-
-        @pl.when(self.z < self.lines - 1)
-        def _():
-            self.up_copy(self.z, self.own).start()
-
-        @pl.when(self.z > 0)
-        def _():
-            self.down_copy(self.z, self.own).start()
-
-        self.across_copy(self.z, self.own).start()
-
-    def wait_line(self, z):
-        block = self.block(z, self.x)
-        self.copy(block, z, self.up, self.from_line, self.z * 2 + 1 - self.x).wait_recv()
+        for h in range(PIECES):
+            pl.when(self.z < self.lines - 1)(lambda: self.up_copy(self.z, h, True).start())
+            pl.when(self.z > 0)(lambda: self.down_copy(self.z, h, True).start())
+            self.across_copy(self.z, h, True).start()
+        self.own_copy().start()
+
+    def wait_line(self, z, h):
+        self.copy(
+            self.block(z, self.x, h), z, h, self.up, self.from_line, self.z * 2 + 1 - self.x
+        ).wait_recv()
 
     def wait_mate(self, z):
-        block = self.block(z, 1 - self.x)
-        pltpu.make_async_remote_copy(
-            src_ref=block, dst_ref=block, send_sem=self.across.at[z], recv_sem=self.from_mate.at[z],
-            device_id={"col": self.z * 2 + 1 - self.x}, device_id_type=MESH,
-        ).wait_recv()
+        for h in range(PIECES):
+            block = self.block(z, 1 - self.x, h)
+            pltpu.make_async_remote_copy(
+                src_ref=block, dst_ref=block, send_sem=self.across.at[z * PIECES + h],
+                recv_sem=self.from_mate.at[z * PIECES + h],
+                device_id={"col": self.z * 2 + 1 - self.x}, device_id_type=MESH,
+            ).wait_recv()
 
     def step(self, s):
-        @pl.when(self.z >= s)
-        def _():
-            z = self.z - s
-            self.wait_line(z)
-            self.across_copy(z, self.block(z, self.x)).start()
-
-            @pl.when(self.z < self.lines - 1)
-            def _():
-                self.up_copy(z, self.block(z, self.x)).start()
-
-        @pl.when(self.z + s < self.lines)
-        def _():
-            z = self.z + s
-            self.wait_line(z)
-            self.across_copy(z, self.block(z, self.x)).start()
-
-            @pl.when(self.z > 0)
-            def _():
-                self.down_copy(z, self.block(z, self.x)).start()
-
-    def wait_own(self):
-        pltpu.make_async_copy(self.own, self.block(self.z, self.x), self.local.at[0]).wait()
-
-    def end(self):
-        for s in range(self.lines):
+        for h in range(PIECES):
             @pl.when(self.z >= s)
             def _():
                 z = self.z - s
-                self.across_copy(z, self.block(z, self.x)).wait_send()
-
-                @pl.when(self.z < self.lines - 1)
-                def _():
-                    self.up_copy(z, self.block(z, self.x)).wait_send()
+                self.wait_line(z, h)
+                pl.when(self.z < self.lines - 1)(lambda: self.up_copy(z, h).start())
+                self.across_copy(z, h).start()
 
             @pl.when(self.z + s < self.lines)
             def _():
                 z = self.z + s
-                if s > 0:
-                    self.across_copy(z, self.block(z, self.x)).wait_send()
-
-                @pl.when(self.z > 0)
+                self.wait_line(z, h)
+                pl.when(self.z > 0)(lambda: self.down_copy(z, h).start())
+                self.across_copy(z, h).start()
+
+    def wait_own(self):
+        self.own_copy().wait()
+
+    def end(self):
+        for s in range(self.lines):
+            for h in range(PIECES):
+                @pl.when(self.z >= s)
                 def _():
-                    self.down_copy(z, self.block(z, self.x)).wait_send()
+                    z = self.z - s
+                    self.across_copy(z, h).wait_send()
+                    pl.when(self.z < self.lines - 1)(lambda: self.up_copy(z, h).wait_send())
+
+                @pl.when(self.z + s < self.lines)
+                def _():
+                    z = self.z + s
+                    if s > 0:
+                        self.across_copy(z, h).wait_send()
+                    pl.when(self.z > 0)(lambda: self.down_copy(z, h).wait_send())
 
 
 class RowGather:
@@ -186,7 +184,7 @@
 
 def col_sems(n):
     lines = n // 2
-    return [pltpu.SemaphoreType.DMA((1,))] + [pltpu.SemaphoreType.DMA((lines,))] * 5
+    return [pltpu.SemaphoreType.DMA((1,))] + [pltpu.SemaphoreType.DMA((lines * PIECES,))] * 5
 
 
 def row_sems(n):
@@ -320,7 +318,7 @@
 
     li.wait_own()
     steps = list(range(1, lines))
-    early = steps[: max(1, len(steps) // 3)]
+    early = steps[: max(1, 2 * len(steps) // 3)]
     for s in early:
         li.step(s)
 
@@ -367,7 +365,7 @@
     rows, f = preact.shape
     tokens = t * n_col
     outer = n_row // 2
-    any_spec = pl.BlockSpec(memory_space=pl.ANY)
+    any_spec = pl.BlockSpec(memory_space=pltpu.HBM)
     return pl.pallas_call(
         functools.partial(hidden_kernel, n_row, n_col),
         out_shape=[
@@ -404,13 +402,50 @@
     )(layer_input, out_grad, preact, weight_out)
 
 
+def col_scatter(n_col, panel, weight):
+    lines = n_col // 2
+    me = lax.axis_index("col")
+    z, x = me // 2, me % 2
+    size = panel.shape[0] // lines
+    rows = size // 2
+    order = np.array([sorted(range(lines), key=lambda t: (-abs(t - p), t)) for p in range(lines)])
+    place = np.argsort(order, axis=1)
+    order, place = jnp.asarray(order, jnp.int32), jnp.asarray(place, jnp.int32)
+    swap = [(i, i + 1 - 2 * (i % 2)) for i in range(n_col)]
+    sums = []
+
+    def of(target):
+        at = place[z, jnp.clip(target, 0, lines - 1)]
+        found = sums[0]
+        for i in range(1, len(sums)):
+            found = jnp.where(at == i, sums[i], found)
+        return found.astype(F32)
+
+    up = down = None
+    for step in range(lines):
+        block = lax.dynamic_slice_in_dim(panel, order[z, step] * size, size, 0)
+        product = width_contract(block, weight).astype(BF16)
+        away = lax.dynamic_slice_in_dim(product, (1 - x) * rows, rows, 0)
+        keep = lax.dynamic_slice_in_dim(product, x * rows, rows, 0)
+        got = lax.ppermute(away, "col", swap)
+        sums.append((keep.astype(F32) + got.astype(F32)).astype(BF16))
+        far = lines - 1 - step
+        going_up, going_down = of(z + far), of(z - far)
+        if step > 0:
+            going_up, going_down = going_up + up.astype(F32), going_down + down.astype(F32)
+        if far > 0:
+            ups = [(2 * p + i, 2 * p + 2 + i) for p in range(step + 1) for i in range(2)]
+            downs = [(n_col - 1 - a, n_col - 1 - b) for a, b in ups]
+            up = lax.ppermute(going_up.astype(BF16), "col", ups)
+            down = lax.ppermute(going_down.astype(BF16), "col", downs)
+    return (going_up + down.astype(F32)).astype(BF16)
+
+
 def local(n_row, n_col, layer_input, out_grad, preact, weight_in, weight_out):
     li_panel, og_panel, act_panel, gp_panel = hidden(
         n_row, n_col, layer_input, out_grad, preact, weight_out
     )
-    input_grad = lax.psum_scatter(
-        width_contract(gp_panel, weight_in).astype(BF16), "col", scatter_dimension=0, tiled=True
-    )
+    input_grad = col_scatter(n_col, gp_panel, weight_in)
     weight_out_grad = token_contract(act_panel, og_panel)
     weight_in_grad = token_contract(li_panel, gp_panel)
     return (input_grad, weight_in_grad, weight_out_grad)

time: 298 us -> 266 us (0.89)
  waiting for transfers between devices: 79.7 us -> 8.92 us
  starting transfers between devices: 0.04 us -> 19.3 us
  matrix products: 55.6 us -> 69.7 us
  other arithmetic: 0.01 us -> 7.62 us
  local copies, waits for them, and re-layouts: 3.5 us -> 9.34 us
  between operations: 14.1 us -> 9.24 us
  Pallas kernels: 145 us -> 141 us
    reduce_scatter x1 -> x0, waiting for transfers between devices: 79.7 us -> none  [local(): lax.psum_scatter(width_contract(gp_panel, weight_in).astype(BF16), 'col',...]
    ppermute x0 -> x10, starting transfers between devices: none -> 19.3 us  [the longest x3 13.1 us: col_scatter(): up = lax.ppermute(going_up.astype(BF16), 'col', ups)]
    dot_general x1 -> x4, matrix products: 18.5 us -> 33.4 us  [width_contract(): lax.dot_general(left, right, (((1,), (1,)), ((), ())), preferred_element_...]
    ppermute x0 -> x10, waiting for transfers between devices: none -> 8.92 us  [the longest x4 7.92 us: col_scatter(): got = lax.ppermute(away, 'col', swap)]
    convert_element_type x0 -> x5, other arithmetic: none -> 7.62 us  [the longest x2 3.8 us: col_scatter(): up = lax.ppermute(going_up.astype(BF16), 'col', ups)]
    pallas_call x1, Pallas kernels: 145 us -> 141 us  [hidden(): pl.pallas_call(functools.partial(hidden_kernel, n_row, n_col), out_shape=...]
    dynamic_slice x0 -> x5, local copies, waits for them, and re-layouts: none -> 3.55 us  [the longest x4 1.99 us: col_scatter(): away = lax.dynamic_slice_in_dim(product, (1 - x) * rows, rows, 0)]
  transfers between devices with their start and end apart: 1 -> 10, of which waited for: 1 -> 2; matrix products, arithmetic and copies ran while one was open for 12% -> 26% of each run, Pallas kernels for 0% -> 0%
where the time goes in v2:
time: 266 us; the launch traced here: 265 us
  Pallas kernels  141 us (53%)
  matrix products  69.7 us (26%)
  starting transfers between devices  19.3 us (7%)
  local copies, waits for them, and re-layouts  9.34 us (4%)
  between operations  9.24 us (3%)
  waiting for transfers between devices  8.92 us (3%)
  other arithmetic  7.62 us (3%)
    pallas_call x1, Pallas kernels, hidden(): pl.pallas_call(functools.partial(hidden_kernel, n_row, n_col), out_shape=...  141 us
    dot_general x2, matrix products, token_contract(): lax.dot_general(left, right, (((0,), (0,)), ((), ())), preferred_element_...  36.3 us
    dot_general x4, matrix products, width_contract(): lax.dot_general(left, right, (((1,), (1,)), ((), ())), preferred_element_...  33.4 us
    ppermute x3, starting transfers between devices, col_scatter(): up = lax.ppermute(going_up.astype(BF16), 'col', ups)  13.1 us
    ppermute x4, waiting for transfers between devices, col_scatter(): got = lax.ppermute(away, 'col', swap)  7.92 us
    unnamed x20, local copies, waits for them, and re-layouts  5.78 us
  transfers between devices with their start and end apart: 10, of which 2 were waited for; matrix products, arithmetic and copies ran while one was open for 26% of the time, Pallas kernels for 0%

profile of v2, /device:TPU:0, one launch (start us, length us, event | category | flops | bytes accessed | tf_op | source)
XLA Modules:
  0.0 264.9 jit_solution(11343760836428080249)
XLA Ops:
  0.7 1.6 constant_dynamic-slice_fusion.6
  2.9 1.2 copy-done
  4.1 1.1 copy-done.1
  5.3 1.1 copy-done.2
  6.4 140.9 %hidden.1 = (bf16[1024,3072]{1,0:T(8,128)(2,1)}, bf16[1024,3072]{1,0:T(8,128)(2,1)}, bf16[1024,2048]{1,0:T(8,128)(2,1)}, bf16[1024,2048]{1,0:T(8,128)(2,1)}) custom-call(bf16[128,3072]{1,0:T(8,128)(2,1)S(1)} %copy-done.1, bf16[128,3072]{1,0:T(8,128)(2,1)S(1)} %copy-done.2, bf16[256,2048]{1,0:T(8,128)(2,1)S(1)} %copy-done, bf16[2048,3072]{1,0:T(8,128)(2,1)} %wo_ref.1), custom_call_target="tpu_custom_call" | custom-call | flops 12884901888 | bytes 54525952 | tf_op jit(solution)/shard_map/hidden/pallas_call | solution.py:369
  147.3 8.4 %convolution_convert_fusion = bf16[256,3072]{1,0:T(8,128)(2,1)S(1)} fusion(bf16[3072,2048]{1,0:T(8,128)(2,1)} %param.10, bf16[1024,2048]{1,0:T(8,128)(2,1)} %get-tuple-element.7, s32[]{:T(128)S(6)} %select_n.118), kind=kOutput, calls=%fused_computation | convolution fusion | flops 3222011904 | bytes 15204356 | tf_op jit(solution)/shard_map/dot_general | solution.py:33
  155.6 1.1 copy-done.3
  158.1 8.4 %convolution_convert_fusion.1 = bf16[256,3072]{1,0:T(8,128)(2,1)S(1)} fusion(bf16[3072,2048]{1,0:T(8,128)(2,1)} %param.10, bf16[1024,2048]{1,0:T(8,128)(2,1)} %get-tuple-element.7, s32[]{:T(128)S(6)} %select_n.117), kind=kOutput, calls=%fused_computation.1 | convolution fusion | flops 3222011904 | bytes 15204356 | tf_op jit(solution)/shard_map/dot_general | solution.py:33
  167.4 1.5 collective-permute-start.2
  169.6 7.9 %collective-permute-done.3 = bf16[128,3072]{1,0:T(8,128)(2,1)} collective-permute-done((bf16[128,3072]{1,0:T(8,128)(2,1)S(1)}, bf16[128,3072]{1,0:T(8,128)(2,1)}, u32[]{:S(2)}, u32[]{:S(2)}) %collective-permute-start.3) | collective-permute-done | bytes 786464 | tf_op jit(solution)/shard_map/ppermute | solution.py:430
  177.5 1.6 add_convert_fusion.5
  179.0 4.4 %collective-permute-start.4 = (bf16[128,3072]{1,0:T(8,128)(2,1)S(1)}, bf16[128,3072]{1,0:T(8,128)(2,1)}, u32[]{:S(2)}, u32[]{:S(2)}) collective-permute-start(bf16[128,3072]{1,0:T(8,128)(2,1)S(1)} %add_convert_fusion.5), channel_id=1, source_target_pairs={{0,2},{1,3},{8,10},{9,11},{16,18},{17,19},{24,26},{25,27}} | collective-permute-start | bytes 2359304 | tf_op jit(solution)/shard_map/ppermute | solution.py:439
  183.5 8.4 %convolution_convert_fusion.2 = bf16[256,3072]{1,0:T(8,128)(2,1)S(1)} fusion(bf16[3072,2048]{1,0:T(8,128)(2,1)} %param.10, bf16[1024,2048]{1,0:T(8,128)(2,1)} %get-tuple-element.7, s32[]{:T(128)S(6)} %select_n.115), kind=kOutput, calls=%fused_computation.2 | convolution fusion | flops 3222011904 | bytes 15204356 | tf_op jit(solution)/shard_map/dot_general | solution.py:33
  191.8 1.1 copy-done.4
  196.5 1.7 add_convert_fusion.4
  198.2 3.7 %collective-permute-start.5 = (bf16[128,3072]{1,0:T(8,128)(2,1)S(1)}, bf16[128,3072]{1,0:T(8,128)(2,1)S(1)}, u32[]{:S(2)}, u32[]{:S(2)}) collective-permute-start(bf16[128,3072]{1,0:T(8,128)(2,1)S(1)} %get-tuple-element.13), channel_id=1, source_target_pairs={{0,2},{1,3},{2,4},{3,5},{8,10},{9,11},{10,12},{11,13},{16,18},{17,... | collective-permute-start | bytes 2359304 | tf_op jit(solution)/shard_map/ppermute | solution.py:439
  201.9 8.4 %convolution_convert_fusion.3 = bf16[256,3072]{1,0:T(8,128)(2,1)S(1)} fusion(bf16[3072,2048]{1,0:T(8,128)(2,1)} %param.10, bf16[1024,2048]{1,0:T(8,128)(2,1)} %get-tuple-element.7, s32[]{:T(128)S(6)} %select_n.110), kind=kOutput, calls=%fused_computation.3 | convolution fusion | flops 3222011904 | bytes 15204356 | tf_op jit(solution)/shard_map/dot_general | solution.py:33
  212.8 1.0 collective-permute-done.5
  213.8 2.1 add_convert_fusion.3
  216.9 19.3 %fusion.11 = f32[2048,3072]{1,0:T(8,128)} fusion(bf16[1024,2048]{1,0:T(8,128)(2,1)S(1)} %copy-done.7, bf16[1024,3072]{1,0:T(8,128)(2,1)} %get-tuple-element.10), kind=kOutput, calls=%fused_computation.32 | convolution fusion | flops 12884901888 | bytes 35651584 | tf_op jit(solution)/shard_map/dot_general | solution.py:27
  237.2 5.0 %collective-permute-start.6 = (bf16[128,3072]{1,0:T(8,128)(2,1)S(1)}, bf16[128,3072]{1,0:T(8,128)(2,1)S(1)}, u32[]{:S(2)}, u32[]{:S(2)}) collective-permute-start(bf16[128,3072]{1,0:T(8,128)(2,1)S(1)} %get-tuple-element.11), channel_id=1, source_target_pairs={{0,2},{1,3},{2,4},{3,5},{4,6},{5,7},{8,10},{9,11},{10,12},{11,13},... | collective-permute-start | bytes 2359304 | tf_op jit(solution)/shard_map/ppermute | solution.py:439
  242.8 1.3 collective-permute-start.9
  244.1 17.0 %fusion.10 = f32[3072,2048]{1,0:T(8,128)} fusion(bf16[1024,3072]{1,0:T(8,128)(2,1)S(1)} %bitcast.22, bf16[1024,2048]{1,0:T(8,128)(2,1)S(1)} %copy-done.6), kind=kOutput, calls=%fused_computation.31 | convolution fusion | flops 12884901888 | bytes 35651584 | tf_op jit(solution)/shard_map/dot_general | solution.py:27
  263.2 1.8 add_convert_fusion
  (34 shorter events, 5.9 us)
Async XLA Ops:
  2.9 1.2 copy-start
  4.1 1.1 copy-start.1
  5.3 1.1 copy-start.2
  155.6 1.1 copy-start.3
  156.8 20.7 %collective-permute-start.3 = (bf16[128,3072]{1,0:T(8,128)(2,1)S(1)}, bf16[128,3072]{1,0:T(8,128)(2,1)}, u32[]{:S(2)}, u32[]{:S(2)}) collective-permute-start(bf16[128,3072]{1,0:T(8,128)(2,1)S(1)} %constant_dynamic-slice_fusion), channel_id=1, source_target_pairs={{0,1},{1,0},{2,3},{3,2},{4,5},{5,4},{6,7},{7,6},{8,9},{9,8},{10,11... | collective-permute-start | bytes 2359304 | tf_op jit(solution)/shard_map/ppermute | solution.py:430
  167.4 29.0 %collective-permute-start.2 = (bf16[128,3072]{1,0:T(8,128)(2,1)}, bf16[128,3072]{1,0:T(8,128)(2,1)S(1)}, u32[]{:S(2)}, u32[]{:S(2)}) collective-permute-start(bf16[128,3072]{1,0:T(8,128)(2,1)} %constant_dynamic-slice_fusion.2), channel_id=1, source_target_pairs={{0,1},{1,0},{2,3},{3,2},{4,5},{5,4},{6,7},{7,6},{8,9},{9,8},{10,11... | collective-permute-start | bytes 2359304 | tf_op jit(solution)/shard_map/ppermute | solution.py:430
  179.0 17.4 %collective-permute-start.4 = (bf16[128,3072]{1,0:T(8,128)(2,1)S(1)}, bf16[128,3072]{1,0:T(8,128)(2,1)}, u32[]{:S(2)}, u32[]{:S(2)}) collective-permute-start(bf16[128,3072]{1,0:T(8,128)(2,1)S(1)} %add_convert_fusion.5), channel_id=1, source_target_pairs={{0,2},{1,3},{8,10},{9,11},{16,18},{17,19},{24,26},{25,27}} | collective-permute-start | bytes 2359304 | tf_op jit(solution)/shard_map/ppermute | solution.py:439
  191.8 1.1 copy-start.4
  193.9 18.9 %collective-permute-start.1 = (bf16[128,3072]{1,0:T(8,128)(2,1)}, bf16[128,3072]{1,0:T(8,128)(2,1)}, u32[]{:S(2)}, u32[]{:S(2)}) collective-permute-start(bf16[128,3072]{1,0:T(8,128)(2,1)} %constant_dynamic-slice_fusion.3), channel_id=1, source_target_pairs={{0,1},{1,0},{2,3},{3,2},{4,5},{5,4},{6,7},{7,6},{8,9},{9,8},{10,11... | collective-permute-start | bytes 2359304 | tf_op jit(solution)/shard_map/ppermute | solution.py:430
  195.7 17.1 %collective-permute-start.7 = (bf16[128,3072]{1,0:T(8,128)(2,1)S(1)}, bf16[128,3072]{1,0:T(8,128)(2,1)S(1)}, u32[]{:S(2)}, u32[]{:S(2)}) collective-permute-start(bf16[128,3072]{1,0:T(8,128)(2,1)S(1)} %add_convert_fusion.5), channel_id=1, source_target_pairs={{7,5},{6,4},{15,13},{14,12},{23,21},{22,20},{31,29},{30,28}} | collective-permute-start | bytes 2359304 | tf_op jit(solution)/shard_map/ppermute | solution.py:440
  198.2 15.6 %copy-start.5 = (bf16[256,3072]{1,0:T(8,128)(2,1)S(1)}, bf16[256,3072]{1,0:T(8,128)(2,1)}, u32[]{:S(2)}) copy-start(bf16[256,3072]{1,0:T(8,128)(2,1)} %copy-done.4) | copy-start | bytes 4718596
  198.2 15.6 %collective-permute-start.5 = (bf16[128,3072]{1,0:T(8,128)(2,1)S(1)}, bf16[128,3072]{1,0:T(8,128)(2,1)S(1)}, u32[]{:S(2)}, u32[]{:S(2)}) collective-permute-start(bf16[128,3072]{1,0:T(8,128)(2,1)S(1)} %get-tuple-element.13), channel_id=1, source_target_pairs={{0,2},{1,3},{2,4},{3,5},{8,10},{9,11},{10,12},{11,13},{16,18},{17,... | collective-permute-start | bytes 2359304 | tf_op jit(solution)/shard_map/ppermute | solution.py:439
  210.3 52.8 %collective-permute-start = (bf16[128,3072]{1,0:T(8,128)(2,1)S(1)}, bf16[128,3072]{1,0:T(8,128)(2,1)S(1)}, u32[]{:S(2)}, u32[]{:S(2)}) collective-permute-start(bf16[128,3072]{1,0:T(8,128)(2,1)S(1)} %constant_dynamic-slice_fusion.4), channel_id=1, source_target_pairs={{0,1},{1,0},{2,3},{3,2},{4,5},{5,4},{6,7},{7,6},{8,9},{9,8},{10,11... | collective-permute-start | bytes 2359304 | tf_op jit(solution)/shard_map/ppermute | solution.py:430
  213.8 3.0 %copy-start.7 = (bf16[1024,2048]{1,0:T(8,128)(2,1)S(1)}, bf16[1024,2048]{1,0:T(8,128)(2,1)}, u32[]{:S(2)}) copy-start(bf16[1024,2048]{1,0:T(8,128)(2,1)} %get-tuple-element.9) | copy-start | bytes 12582916
  215.9 26.4 %collective-permute-start.8 = (bf16[128,3072]{1,0:T(8,128)(2,1)S(1)}, bf16[128,3072]{1,0:T(8,128)(2,1)S(1)}, u32[]{:S(2)}, u32[]{:S(2)}) collective-permute-start(bf16[128,3072]{1,0:T(8,128)(2,1)S(1)} %get-tuple-element.15), channel_id=1, source_target_pairs={{7,5},{6,4},{5,3},{4,2},{15,13},{14,12},{13,11},{12,10},{23,21},{2... | collective-permute-start | bytes 2359304 | tf_op jit(solution)/shard_map/ppermute | solution.py:440
  216.8 27.2 %slice-start = ((s8[6291456]{0:T(1024)(128)(4,1)}), s8[4194304]{0:T(1024)(128)(4,1)S(1)}, s32[]{:S(2)}) async-start(s8[6291456]{0:T(1024)(128)(4,1)} %bitcast.21), calls=%async_computation | async-start | bytes 8388608
  216.9 27.2 %copy-start.6 = (bf16[1024,2048]{1,0:T(8,128)(2,1)S(1)}, bf16[1024,2048]{1,0:T(8,128)(2,1)}, u32[]{:S(2)}) copy-start(bf16[1024,2048]{1,0:T(8,128)(2,1)} %get-tuple-element.7) | copy-start | bytes 12582916
  216.9 27.2 %slice-start.1 = ((s8[6291456]{0:T(1024)(128)(4,1)}), s8[2097152]{0:T(1024)(128)(4,1)S(1)}, s32[]{:S(2)}) async-start(s8[6291456]{0:T(1024)(128)(4,1)} %bitcast.21), calls=%async_computation.1 | async-start | bytes 4194304
  237.2 25.9 %collective-permute-start.6 = (bf16[128,3072]{1,0:T(8,128)(2,1)S(1)}, bf16[128,3072]{1,0:T(8,128)(2,1)S(1)}, u32[]{:S(2)}, u32[]{:S(2)}) collective-permute-start(bf16[128,3072]{1,0:T(8,128)(2,1)S(1)} %get-tuple-element.11), channel_id=1, source_target_pairs={{0,2},{1,3},{2,4},{3,5},{4,6},{5,7},{8,10},{9,11},{10,12},{11,13},... | collective-permute-start | bytes 2359304 | tf_op jit(solution)/shard_map/ppermute | solution.py:439
  242.8 20.4 %collective-permute-start.9 = (bf16[128,3072]{1,0:T(8,128)(2,1)S(1)}, bf16[128,3072]{1,0:T(8,128)(2,1)S(1)}, u32[]{:S(2)}, u32[]{:S(2)}) collective-permute-start(bf16[128,3072]{1,0:T(8,128)(2,1)S(1)} %add_convert_fusion.1), channel_id=1, source_target_pairs={{7,5},{6,4},{5,3},{4,2},{3,1},{2,0},{15,13},{14,12},{13,11},{12,10... | collective-permute-start | bytes 2359304 | tf_op jit(solution)/shard_map/ppermute | solution.py:440

commit v3 on v2

--- a/solution.py
+++ b/solution.py
@@ -220,13 +220,14 @@
 
 STRIP = 16
 COLS = 256
+TALL = 512
 
 
 def hidden_kernel(
     n_row, n_col,
-    li_ref, og_ref, pre_ref, wo_ref,
-    li_panel, og_panel, act_panel, gp_panel,
-    wo, pair, part, pre, act, slope, first, second, outgoing, own_gp,
+    li_ref, og_ref, pre_ref, wi_ref, wo_ref,
+    li_panel, og_panel, act_panel, gp_panel, out_panel,
+    wi, wo, pair, part, product, pre, act, slope, first, second, outgoing, own_gp,
     load_sem, s1_send, s1_recv, s2_send, s2_recv, *sems,
 ):
     og = ColGather(n_col, og_ref, og_panel, sems[0:6])
@@ -244,6 +245,8 @@
     load_pre.start()
     load_wo = pltpu.make_async_copy(wo_ref, wo, load_sem.at[1])
     load_wo.start()
+    load_wi = pltpu.make_async_copy(wi_ref, wi, load_sem.at[3])
+    load_wi.start()
 
     load_pre.wait()
 
@@ -271,21 +274,6 @@
             k = pl.ds(pl.multiple_of(j * COLS, COLS), COLS)
             part[pl.ds(start, size), k] = width_contract(pair[...], wo[k, :]).astype(BF16)
 
-    def multiply_step(s):
-        if s == 0:
-            multiply(og.z)
-        else:
-            pl.when(og.z >= s)(lambda: multiply(og.z - s))
-            pl.when(og.z + s < lines)(lambda: multiply(og.z + s))
-
-    for s in range(1, lines):
-        og.step(s)
-        if s == lines - 1:
-            li.start()
-        multiply_step(s - 1)
-    act_rows.forward()
-    multiply_step(lines - 1)
-
     def own_rows(q):
         return pl.ds(pl.multiple_of(q * rows, rows), rows)
 
@@ -302,54 +290,106 @@
         )
 
     order = [(o + k) % outer for k in range(1, outer)] + [o]
-    for k in order:
-        first_copy(k).start()
-    for k in order[:-1]:
-        first_copy(k).wait_recv()
-
-        @pl.loop(0, rows // STRIP)
-        def _(i):
-            at = pl.multiple_of(i * STRIP, STRIP)
-            mine = part[pl.ds(pl.multiple_of((k * 2 + c) * rows + at, STRIP), STRIP), :]
-            r = pl.ds(at, STRIP)
-            outgoing[k, r, :] = (mine.astype(F32) + first[k, r, :].astype(F32)).astype(BF16)
-
-        second_copy(k).start()
-
+    owners = 2 * og.rows // rows
+
+    def exchange(z):
+        for i in range(owners):
+            q = z * owners + i
+            k, kc = q // 2, q % 2
+            pl.when(c != kc)(lambda: first_copy(k).start())
+        for i in range(owners):
+            q = z * owners + i
+            k, kc = q // 2, q % 2
+
+            @pl.when(c == kc)
+            def _():
+                first_copy(k).wait_recv()
+
+                @pl.when(o != k)
+                def _():
+                    @pl.loop(0, rows // STRIP)
+                    def _(i):
+                        at = pl.multiple_of(i * STRIP, STRIP)
+                        mine = part[pl.ds(pl.multiple_of(q * rows + at, STRIP), STRIP), :]
+                        r = pl.ds(at, STRIP)
+                        outgoing[k, r, :] = (mine.astype(F32) + first[k, r, :].astype(F32)).astype(BF16)
+
+                    second_copy(k).start()
+
+    def finish(z):
+        @pl.when(me // owners == z)
+        def _():
+            for k in order[:-1]:
+                pltpu.make_async_remote_copy(
+                    src_ref=outgoing.at[k], dst_ref=second.at[k], send_sem=s2_send.at[k],
+                    recv_sem=s2_recv.at[k], device_id={"row": k * 2 + c}, device_id_type=MESH,
+                ).wait_recv()
+
+            @pl.loop(0, rows // STRIP)
+            def _(i):
+                at = pl.multiple_of(i * STRIP, STRIP)
+                r = pl.ds(at, STRIP)
+                total = part[pl.ds(pl.multiple_of(me * rows + at, STRIP), STRIP), :].astype(F32)
+                total = total + first[o, r, :].astype(F32)
+                for k in order[:-1]:
+                    total = total + second[k, r, :].astype(F32)
+                own_gp[r, :] = (total * slope[r, :]).astype(BF16)
+
+            gp_rows.start()
+
+    def at_step(s, act_on):
+        if s == 0:
+            act_on(og.z)
+        elif s > 0:
+            pl.when(og.z >= s)(lambda: act_on(og.z - s))
+            pl.when(og.z + s < lines)(lambda: act_on(og.z + s))
+
+    def multiply_and_exchange(z):
+        multiply(z)
+        exchange(z)
+
+    for s in range(1, lines):
+        og.step(s)
+        if s == lines - 1:
+            li.start()
+        at_step(s - 1, multiply_and_exchange)
+        at_step(s - 2, finish)
+    act_rows.forward()
+    at_step(lines - 1, multiply_and_exchange)
     li.wait_own()
     steps = list(range(1, lines))
     early = steps[: max(1, 2 * len(steps) // 3)]
-    for s in early:
+    li.step(1)
+    at_step(lines - 2, finish)
+    for s in early[1:]:
         li.step(s)
-
-    first_copy(o).wait_recv()
-    for k in order[:-1]:
-        pltpu.make_async_remote_copy(
-            src_ref=outgoing.at[k], dst_ref=second.at[k], send_sem=s2_send.at[k],
-            recv_sem=s2_recv.at[k], device_id={"row": k * 2 + c}, device_id_type=MESH,
-        ).wait_recv()
-
-    @pl.loop(0, rows // STRIP)
-    def _(i):
-        at = pl.multiple_of(i * STRIP, STRIP)
-        r = pl.ds(at, STRIP)
-        total = part[pl.ds(pl.multiple_of(me * rows + at, STRIP), STRIP), :].astype(F32)
-        total = total + first[o, r, :].astype(F32)
-        for k in order[:-1]:
-            total = total + second[k, r, :].astype(F32)
-        own_gp[r, :] = (total * slope[r, :]).astype(BF16)
-
-    gp_rows.start()
+    at_step(lines - 1, finish)
     for s in steps[len(early):]:
         li.step(s)
     gp_rows.forward()
-
     for k in order:
         first_copy(k).wait_send()
+    gp_rows.end()
+    fetch_gp = pltpu.make_async_copy(gp_panel, part, load_sem.at[2])
+    fetch_gp.start()
+    load_wi.wait()
+    fetch_gp.wait()
+
+    @pl.loop(0, part.shape[0] // TALL)
+    def _(i):
+        r = pl.ds(pl.multiple_of(i * TALL, TALL), TALL)
+
+        @pl.loop(0, wi.shape[0] // COLS)
+        def _(j):
+            k = pl.ds(pl.multiple_of(j * COLS, COLS), COLS)
+            product[r, k] = width_contract(part[r, :], wi[k, :]).astype(BF16)
+
+    store = pltpu.make_async_copy(product, out_panel, load_sem.at[2])
+    store.start()
+
     for k in order[:-1]:
         second_copy(k).wait_send()
     act_rows.end()
-    gp_rows.end()
     og.end()
     for s in range(lines):
         if s == 0:
@@ -358,9 +398,10 @@
             pl.when(li.z >= s)(lambda: li.wait_mate(li.z - s))
             pl.when(li.z + s < lines)(lambda: li.wait_mate(li.z + s))
     li.end()
-
-
-def hidden(n_row, n_col, layer_input, out_grad, preact, weight_out):
+    store.wait()
+
+
+def hidden(n_row, n_col, layer_input, out_grad, preact, weight_in, weight_out):
     t, d = layer_input.shape
     rows, f = preact.shape
     tokens = t * n_col
@@ -373,13 +414,16 @@
             jax.ShapeDtypeStruct((tokens, d), BF16),
             jax.ShapeDtypeStruct((tokens, f), BF16),
             jax.ShapeDtypeStruct((tokens, f), BF16),
+            jax.ShapeDtypeStruct((tokens, d), BF16),
         ],
-        in_specs=[any_spec] * 4,
-        out_specs=[any_spec] * 4,
+        in_specs=[any_spec] * 5,
+        out_specs=[any_spec] * 5,
         scratch_shapes=[
+            pltpu.VMEM((d, f), BF16),
             pltpu.VMEM((f, d), BF16),
             pltpu.VMEM((2 * t, d), BF16),
             pltpu.VMEM((tokens, f), BF16),
+            pltpu.VMEM((tokens, d), BF16),
             pltpu.VMEM((rows, f), BF16),
             pltpu.VMEM((rows, f), BF16),
             pltpu.VMEM((rows, f), F32),
@@ -387,27 +431,26 @@
             pltpu.VMEM((outer, rows, f), BF16),
             pltpu.VMEM((outer, rows, f), BF16),
             pltpu.VMEM((rows, f), BF16),
-            pltpu.SemaphoreType.DMA((3,)),
+            pltpu.SemaphoreType.DMA((4,)),
         ]
         + [pltpu.SemaphoreType.DMA((outer,))] * 4
         + col_sems(n_col) * 2
         + row_sems(n_row) * 2,
         compiler_params=pltpu.CompilerParams(
-            collective_id=0, has_side_effects=True, vmem_limit_bytes=50 * 2**20
+            collective_id=0, has_side_effects=True, vmem_limit_bytes=58 * 2**20
         ),
         cost_estimate=pl.CostEstimate(
-            flops=2 * tokens * d * f, bytes_accessed=2 * (f * d + 4 * tokens * (d + f)), transcendentals=rows * f
+            flops=4 * tokens * d * f, bytes_accessed=4 * (f * d + 2 * tokens * (d + f)), transcendentals=rows * f
         ),
         name="hidden",
-    )(layer_input, out_grad, preact, weight_out)
-
-
-def col_scatter(n_col, panel, weight):
+    )(layer_input, out_grad, preact, weight_in, weight_out)
+
+
+def col_scatter(n_col, panel, others):
     lines = n_col // 2
     me = lax.axis_index("col")
     z, x = me // 2, me % 2
-    size = panel.shape[0] // lines
-    rows = size // 2
+    rows = panel.shape[0] // n_col
     order = np.array([sorted(range(lines), key=lambda t: (-abs(t - p), t)) for p in range(lines)])
     place = np.argsort(order, axis=1)
     order, place = jnp.asarray(order, jnp.int32), jnp.asarray(place, jnp.int32)
@@ -423,10 +466,11 @@
 
     up = down = None
     for step in range(lines):
-        block = lax.dynamic_slice_in_dim(panel, order[z, step] * size, size, 0)
-        product = width_contract(block, weight).astype(BF16)
-        away = lax.dynamic_slice_in_dim(product, (1 - x) * rows, rows, 0)
-        keep = lax.dynamic_slice_in_dim(product, x * rows, rows, 0)
+        at = order[z, step] * 2
+        away = lax.dynamic_slice_in_dim(panel, (at + 1 - x) * rows, rows, 0)
+        keep = lax.dynamic_slice_in_dim(panel, (at + x) * rows, rows, 0)
+        if step in others:
+            keep, others[step] = lax.optimization_barrier((keep, others[step]))
         got = lax.ppermute(away, "col", swap)
         sums.append((keep.astype(F32) + got.astype(F32)).astype(BF16))
         far = lines - 1 - step
@@ -438,17 +482,16 @@
             downs = [(n_col - 1 - a, n_col - 1 - b) for a, b in ups]
             up = lax.ppermute(going_up.astype(BF16), "col", ups)
             down = lax.ppermute(going_down.astype(BF16), "col", downs)
-    return (going_up + down.astype(F32)).astype(BF16)
+    return (going_up + down.astype(F32)).astype(BF16), others
 
 
 def local(n_row, n_col, layer_input, out_grad, preact, weight_in, weight_out):
-    li_panel, og_panel, act_panel, gp_panel = hidden(
-        n_row, n_col, layer_input, out_grad, preact, weight_out
+    li_panel, og_panel, act_panel, gp_panel, out_panel = hidden(
+        n_row, n_col, layer_input, out_grad, preact, weight_in, weight_out
     )
-    input_grad = col_scatter(n_col, gp_panel, weight_in)
-    weight_out_grad = token_contract(act_panel, og_panel)
-    weight_in_grad = token_contract(li_panel, gp_panel)
-    return (input_grad, weight_in_grad, weight_out_grad)
+    beside = {0: token_contract(act_panel, og_panel), 2: token_contract(li_panel, gp_panel)}
+    input_grad, beside = col_scatter(n_col, out_panel, beside)
+    return (input_grad, beside[2], beside[0])
 
 
 def solution(mesh):

time: 266 us -> 265 us (level)
  matrix products: 69.7 us -> 38.1 us
  Pallas kernels: 141 us -> 158 us
  waiting for transfers between devices: 8.92 us -> 23.5 us
  local copies, waits for them, and re-layouts: 9.34 us -> 5.6 us
    dot_general x4 -> x0, matrix products: 33.4 us -> none  [width_contract(): lax.dot_general(left, right, (((1,), (1,)), ((), ())), preferred_element_...]
    pallas_call x1, Pallas kernels: 141 us -> 158 us  [hidden(): pl.pallas_call(functools.partial(hidden_kernel, n_row, n_col), out_shape=...]
    ppermute x3, waiting for transfers between devices: 0.01 us -> 11.4 us  [col_scatter(): down = lax.ppermute(going_down.astype(BF16), 'col', downs)]
    unnamed x20 -> x6, local copies, waits for them, and re-layouts: 5.78 us -> 0.01 us
    ppermute x3, waiting for transfers between devices: 1 us -> 3.67 us  [col_scatter(): up = lax.ppermute(going_up.astype(BF16), 'col', ups)]
    dynamic_slice x5 -> x2, local copies, waits for them, and re-layouts: 3.55 us -> 5.59 us  [the longest x1 4.03 us: col_scatter(): away = lax.dynamic_slice_in_dim(panel, (at + 1 - x) * rows, rows, 0)]
  transfers between devices with their start and end apart: 10 -> 10, of which waited for: 2 -> 4; matrix products, arithmetic and copies ran while one was open for 26% -> 17% of each run, Pallas kernels for 0% -> 0%
where the time goes in v3:
time: 265 us; the launch traced here: 264 us
  Pallas kernels  158 us (60%)
  matrix products  38.1 us (14%)
  waiting for transfers between devices  23.5 us (9%)
  starting transfers between devices  20.6 us (8%)
  other arithmetic  9.69 us (4%)
  between operations  8.77 us (3%)
  local copies, waits for them, and re-layouts  5.6 us (2%)
    pallas_call x1, Pallas kernels, hidden(): pl.pallas_call(functools.partial(hidden_kernel, n_row, n_col), out_shape=...  158 us
    dot_general x2, matrix products, token_contract(): lax.dot_general(left, right, (((0,), (0,)), ((), ())), preferred_element_...  38.1 us
    ppermute x3, starting transfers between devices, col_scatter(): up = lax.ppermute(going_up.astype(BF16), 'col', ups)  12.8 us
    ppermute x3, waiting for transfers between devices, col_scatter(): down = lax.ppermute(going_down.astype(BF16), 'col', downs)  11.4 us
    ppermute x4, waiting for transfers between devices, col_scatter(): got = lax.ppermute(away, 'col', swap)  8.44 us
  transfers between devices with their start and end apart: 10, of which 4 were waited for; matrix products, arithmetic and copies ran while one was open for 17% of the time, Pallas kernels for 0%

profile of v3, /device:TPU:0, one launch (start us, length us, event | category | flops | bytes accessed | tf_op | source)
XLA Modules:
  0.0 264.0 jit_solution(12845244125861019440)
XLA Ops:
  0.7 1.6 constant_dynamic-slice_fusion.8
  4.8 157.7 %hidden.1 = (bf16[1024,3072]{1,0:T(8,128)(2,1)}, bf16[1024,3072]{1,0:T(8,128)(2,1)}, bf16[1024,2048]{1,0:T(8,128)(2,1)}, bf16[1024,2048]{1,0:T(8,128)(2,1)}, bf16[1024,3072]{1,0:T(8,128)(2,1)}) custom-call(bf16[128,3072]{1,0:T(8,128)(2,1)} %li_ref.1, bf16[128,3072]{1,0:T(8,128)(2,1)} %og_ref.1, bf16[256,2048]{1,0:T(8,128)(2,1)} %pre_ref.1, ...), custom_call_target="tpu_custom_call" | custom-call | flops 25769803776 | bytes 67108864 | tf_op jit(solution)/shard_map/hidden/pallas_call | solution.py:410
  162.5 4.0 %constant_dynamic-slice_fusion.6 = (bf16[128,3072]{1,0:T(8,128)(2,1)}, bf16[128,3072]{1,0:T(8,128)(2,1)S(1)}, bf16[128,3072]{1,0:T(8,128)(2,1)S(1)}, bf16[128,30...) fusion(bf16[1024,3072]{1,0:T(8,128)(2,1)} %get-tuple-element.12, s32[]{:T(128)S(6)} %select_n.112, ...), kind=kLoop, calls=%fused_computation.16 | loop fusion | bytes 9437208 | tf_op jit(solution)/shard_map/dynamic_slice | solution.py:470
  166.5 0.5 collective-permute-start.3
  167.1 1.5 collective-permute-start.2
  168.6 19.2 %fusion.3 = f32[2048,3072]{1,0:T(8,128)} fusion(bf16[1024,2048]{1,0:T(8,128)(2,1)} %get-tuple-element.16, bf16[1024,3072]{1,0:T(8,128)(2,1)S(1)} %copy-done.1), kind=kOutput, calls=%fused_computation.22 | convolution fusion | flops 12884901888 | bytes 35651584 | tf_op jit(solution)/shard_map/dot_general | solution.py:27
  187.7 0.2 add_convert_fusion.5
  187.9 2.6 collective-permute-start.4
  190.5 1.6 collective-permute-start.7
  192.1 0.5 collective-permute-start.1
  192.6 1.5 collective-permute-start
  195.3 8.4 %collective-permute-done.2 = bf16[128,3072]{1,0:T(8,128)(2,1)S(1)} collective-permute-done((bf16[128,3072]{1,0:T(8,128)(2,1)}, bf16[128,3072]{1,0:T(8,128)(2,1)S(1)}, u32[]{:S(2)}, u32[]{:S(2)}) %collective-permute-start.2) | collective-permute-done | bytes 786464 | tf_op jit(solution)/shard_map/ppermute | solution.py:474
  203.7 2.5 collective-permute-done.4
  206.2 2.3 add_convert_fusion.4
  208.5 4.7 %collective-permute-start.5 = (bf16[128,3072]{1,0:T(8,128)(2,1)S(1)}, bf16[128,3072]{1,0:T(8,128)(2,1)S(1)}, u32[]{:S(2)}, u32[]{:S(2)}) collective-permute-start(bf16[128,3072]{1,0:T(8,128)(2,1)S(1)} %get-tuple-element.21), channel_id=1, source_target_pairs={{0,2},{1,3},{2,4},{3,5},{8,10},{9,11},{10,12},{11,13},{16,18},{17,... | collective-permute-start | bytes 2359304 | tf_op jit(solution)/shard_map/ppermute | solution.py:483
  213.2 1.5 add_convert_fusion.2
  214.7 0.9 collective-permute-start.8
  215.7 19.0 %fusion.2 = f32[3072,2048]{1,0:T(8,128)} fusion(bf16[1024,3072]{1,0:T(8,128)(2,1)S(1)} %copy-done.2, bf16[1024,2048]{1,0:T(8,128)(2,1)} %get-tuple-element.14), kind=kOutput, calls=%fused_computation.21 | convolution fusion | flops 12884901888 | bytes 35651584 | tf_op jit(solution)/shard_map/dot_general | solution.py:27
  237.0 2.0 add_convert_fusion.3
  238.9 1.3 collective-permute-start.9
  240.2 5.5 %collective-permute-start.6 = (bf16[128,3072]{1,0:T(8,128)(2,1)}, bf16[128,3072]{1,0:T(8,128)(2,1)}, u32[]{:S(2)}, u32[]{:S(2)}) collective-permute-start(bf16[128,3072]{1,0:T(8,128)(2,1)} %get-tuple-element.29), channel_id=1, source_target_pairs={{0,2},{1,3},{2,4},{3,5},{4,6},{5,7},{8,10},{9,11},{10,12},{11,13},... | collective-permute-start | bytes 2359304 | tf_op jit(solution)/shard_map/ppermute | solution.py:483
  247.7 11.4 %collective-permute-done.9 = bf16[128,3072]{1,0:T(8,128)(2,1)} collective-permute-done((bf16[128,3072]{1,0:T(8,128)(2,1)}, bf16[128,3072]{1,0:T(8,128)(2,1)}, u32[]{:S(2)}, u32[]{:S(2)}) %collective-permute-start.9) | collective-permute-done | bytes 786464 | tf_op jit(solution)/shard_map/ppermute | solution.py:484
  259.1 1.2 collective-permute-done.6
  260.2 3.7 %add_convert_fusion = bf16[128,3072]{1,0:T(8,128)(2,1)} fusion(bf16[128,3072]{1,0:T(8,128)(2,1)} %collective-permute-done.9, bf16[128,3072]{1,0:T(8,128)(2,1)} %collective-permute-done.6, bf16[128,3072]{1,0:T(8,128)(2,1)} %collective-permute-done, bf16[128,3072]{1,0:T(8,128)(2,1)S(1)} %get-tuple-element.22, bf16[128,3072]{1,0:T(8,128)(2,1)S(1)} %add_convert_fusion.5, ...), kind=kLoop, calls=%fused_computation | loop fusion | flops 6684672 | bytes 7077895 | tf_op jit(solution)/shard_map/convert_element_type | solution.py:485
  (12 shorter events, 0.0 us)
Async XLA Ops:
  162.5 6.1 %copy-start.1 = (bf16[1024,3072]{1,0:T(8,128)(2,1)S(1)}, bf16[1024,3072]{1,0:T(8,128)(2,1)}, u32[]{:S(2)}) copy-start(bf16[1024,3072]{1,0:T(8,128)(2,1)} %get-tuple-element.17) | copy-start | bytes 18874372
  166.5 21.2 %collective-permute-start.3 = (bf16[128,3072]{1,0:T(8,128)(2,1)S(1)}, bf16[128,3072]{1,0:T(8,128)(2,1)S(1)}, u32[]{:S(2)}, u32[]{:S(2)}) collective-permute-start(bf16[128,3072]{1,0:T(8,128)(2,1)S(1)} %get-tuple-element.24), channel_id=1, source_target_pairs={{0,1},{1,0},{2,3},{3,2},{4,5},{5,4},{6,7},{7,6},{8,9},{9,8},{10,11... | collective-permute-start | bytes 2359304 | tf_op jit(solution)/shard_map/ppermute | solution.py:474
  167.1 36.7 %collective-permute-start.2 = (bf16[128,3072]{1,0:T(8,128)(2,1)}, bf16[128,3072]{1,0:T(8,128)(2,1)S(1)}, u32[]{:S(2)}, u32[]{:S(2)}) collective-permute-start(bf16[128,3072]{1,0:T(8,128)(2,1)} %get-tuple-element.26), channel_id=1, source_target_pairs={{0,1},{1,0},{2,3},{3,2},{4,5},{5,4},{6,7},{7,6},{8,9},{9,8},{10,11... | collective-permute-start | bytes 2359304 | tf_op jit(solution)/shard_map/ppermute | solution.py:474
  187.9 18.3 %collective-permute-start.4 = (bf16[128,3072]{1,0:T(8,128)(2,1)S(1)}, bf16[128,3072]{1,0:T(8,128)(2,1)}, u32[]{:S(2)}, u32[]{:S(2)}) collective-permute-start(bf16[128,3072]{1,0:T(8,128)(2,1)S(1)} %add_convert_fusion.5), channel_id=1, source_target_pairs={{0,2},{1,3},{8,10},{9,11},{16,18},{17,19},{24,26},{25,27}} | collective-permute-start | bytes 2359304 | tf_op jit(solution)/shard_map/ppermute | solution.py:483
  190.5 22.7 %collective-permute-start.7 = (bf16[128,3072]{1,0:T(8,128)(2,1)S(1)}, bf16[128,3072]{1,0:T(8,128)(2,1)}, u32[]{:S(2)}, u32[]{:S(2)}) collective-permute-start(bf16[128,3072]{1,0:T(8,128)(2,1)S(1)} %add_convert_fusion.5), channel_id=1, source_target_pairs={{7,5},{6,4},{15,13},{14,12},{23,21},{22,20},{31,29},{30,28}} | collective-permute-start | bytes 2359304 | tf_op jit(solution)/shard_map/ppermute | solution.py:484
  192.1 44.9 %collective-permute-start.1 = (bf16[128,3072]{1,0:T(8,128)(2,1)}, bf16[128,3072]{1,0:T(8,128)(2,1)S(1)}, u32[]{:S(2)}, u32[]{:S(2)}) collective-permute-start(bf16[128,3072]{1,0:T(8,128)(2,1)} %get-tuple-element.27), channel_id=1, source_target_pairs={{0,1},{1,0},{2,3},{3,2},{4,5},{5,4},{6,7},{7,6},{8,9},{9,8},{10,11... | collective-permute-start | bytes 2359304 | tf_op jit(solution)/shard_map/ppermute | solution.py:474
  192.6 55.0 %collective-permute-start = (bf16[128,3072]{1,0:T(8,128)(2,1)}, bf16[128,3072]{1,0:T(8,128)(2,1)}, u32[]{:S(2)}, u32[]{:S(2)}) collective-permute-start(bf16[128,3072]{1,0:T(8,128)(2,1)} %get-tuple-element.23), channel_id=1, source_target_pairs={{0,1},{1,0},{2,3},{3,2},{4,5},{5,4},{6,7},{7,6},{8,9},{9,8},{10,11... | collective-permute-start | bytes 2359304 | tf_op jit(solution)/shard_map/ppermute | solution.py:474
  203.7 2.5 copy-start
  206.2 9.4 %copy-start.2 = (bf16[1024,3072]{1,0:T(8,128)(2,1)S(1)}, bf16[1024,3072]{1,0:T(8,128)(2,1)}, u32[]{:S(2)}) copy-start(bf16[1024,3072]{1,0:T(8,128)(2,1)} %get-tuple-element.13) | copy-start | bytes 18874372
  208.5 28.4 %collective-permute-start.5 = (bf16[128,3072]{1,0:T(8,128)(2,1)S(1)}, bf16[128,3072]{1,0:T(8,128)(2,1)S(1)}, u32[]{:S(2)}, u32[]{:S(2)}) collective-permute-start(bf16[128,3072]{1,0:T(8,128)(2,1)S(1)} %get-tuple-element.21), channel_id=1, source_target_pairs={{0,2},{1,3},{2,4},{3,5},{8,10},{9,11},{10,12},{11,13},{16,18},{17,... | collective-permute-start | bytes 2359304 | tf_op jit(solution)/shard_map/ppermute | solution.py:483
  214.7 22.2 %collective-permute-start.8 = (bf16[128,3072]{1,0:T(8,128)(2,1)S(1)}, bf16[128,3072]{1,0:T(8,128)(2,1)S(1)}, u32[]{:S(2)}, u32[]{:S(2)}) collective-permute-start(bf16[128,3072]{1,0:T(8,128)(2,1)S(1)} %add_convert_fusion.2), channel_id=1, source_target_pairs={{7,5},{6,4},{5,3},{4,2},{15,13},{14,12},{13,11},{12,10},{23,21},{2... | collective-permute-start | bytes 2359304 | tf_op jit(solution)/shard_map/ppermute | solution.py:484
  238.9 20.1 %collective-permute-start.9 = (bf16[128,3072]{1,0:T(8,128)(2,1)}, bf16[128,3072]{1,0:T(8,128)(2,1)}, u32[]{:S(2)}, u32[]{:S(2)}) collective-permute-start(bf16[128,3072]{1,0:T(8,128)(2,1)} %get-tuple-element.30), channel_id=1, source_target_pairs={{7,5},{6,4},{5,3},{4,2},{3,1},{2,0},{15,13},{14,12},{13,11},{12,10... | collective-permute-start | bytes 2359304 | tf_op jit(solution)/shard_map/ppermute | solution.py:484
  240.2 20.0 %collective-permute-start.6 = (bf16[128,3072]{1,0:T(8,128)(2,1)}, bf16[128,3072]{1,0:T(8,128)(2,1)}, u32[]{:S(2)}, u32[]{:S(2)}) collective-permute-start(bf16[128,3072]{1,0:T(8,128)(2,1)} %get-tuple-element.29), channel_id=1, source_target_pairs={{0,2},{1,3},{2,4},{3,5},{4,6},{5,7},{8,10},{9,11},{10,12},{11,13},... | collective-permute-start | bytes 2359304 | tf_op jit(solution)/shard_map/ppermute | solution.py:483

commit v4 on v3

--- a/solution.py
+++ b/solution.py
@@ -168,8 +168,33 @@
             ).wait_recv()
             self.across_copy(o, block).start()
 
+    def wait_own(self):
+        pltpu.make_async_copy(self.own, self.block(self.o, self.c), self.local.at[0]).wait()
+
+    def pass_on(self, o):
+        block = self.block(o, self.c)
+        pltpu.make_async_remote_copy(
+            src_ref=block, dst_ref=block, send_sem=self.far.at[o], recv_sem=self.from_far.at[o],
+            device_id={"row": o * 2 + self.c}, device_id_type=MESH,
+        ).wait_recv()
+        self.across_copy(o, block).start()
+
+    def wait_mate(self, o):
+        block = self.block(o, 1 - self.c)
+        pltpu.make_async_remote_copy(
+            src_ref=block, dst_ref=block, send_sem=self.across.at[o], recv_sem=self.from_mate.at[o],
+            device_id={"row": self.o * 2 + 1 - self.c}, device_id_type=MESH,
+        ).wait_recv()
+
+    def wait_sends(self):
+        for k in range(1, self.outer):
+            self.far_copy((self.o + k) % self.outer).wait_send()
+        for k in range(self.outer):
+            o = (self.o + k) % self.outer
+            self.across_copy(o, self.block(o, self.c)).wait_send()
+
     def end(self):
-        pltpu.make_async_copy(self.own, self.block(self.o, self.c), self.local.at[0]).wait()
+        self.wait_own()
         for k in range(1, self.outer):
             self.far_copy((self.o + k) % self.outer).wait_send()
         for k in range(self.outer):
@@ -220,14 +245,13 @@
 
 STRIP = 16
 COLS = 256
-TALL = 512
 
 
 def hidden_kernel(
     n_row, n_col,
     li_ref, og_ref, pre_ref, wi_ref, wo_ref,
     li_panel, og_panel, act_panel, gp_panel, out_panel,
-    wi, wo, pair, part, product, pre, act, slope, first, second, outgoing, own_gp,
+    wi, wo, pair, gp_pair, part, product, pre, act, slope, first, second, outgoing, own_gp,
     load_sem, s1_send, s1_recv, s2_send, s2_recv, *sems,
 ):
     og = ColGather(n_col, og_ref, og_panel, sems[0:6])
@@ -356,7 +380,30 @@
         at_step(s - 2, finish)
     act_rows.forward()
     at_step(lines - 1, multiply_and_exchange)
+    def gp_ready(z):
+        for i in range(owners):
+            q = z * owners + i
+            k, kc = q // 2, q % 2
+            pl.when(q == me)(lambda: gp_rows.wait_own())
+            pl.when((c == kc) & (o != k))(lambda: gp_rows.pass_on(k))
+            pl.when(c != kc)(lambda: gp_rows.wait_mate(k))
+
+    def multiply_back(z):
+        size = 2 * og.rows
+        start = pl.multiple_of(z * size, size)
+        gp_ready(z)
+        fetch = pltpu.make_async_copy(gp_panel.at[pl.ds(start, size)], gp_pair, load_sem.at[2])
+        fetch.start()
+        fetch.wait()
+
+        @pl.loop(0, wi.shape[0] // COLS)
+        def _(j):
+            k = pl.ds(pl.multiple_of(j * COLS, COLS), COLS)
+            product[pl.ds(start, size), k] = width_contract(gp_pair[...], wi[k, :]).astype(BF16)
+
     li.wait_own()
+    load_wi.wait()
+    at_step(0, multiply_back)
     steps = list(range(1, lines))
     early = steps[: max(1, 2 * len(steps) // 3)]
     li.step(1)
@@ -364,25 +411,14 @@
     for s in early[1:]:
         li.step(s)
     at_step(lines - 1, finish)
+    at_step(1, multiply_back)
     for s in steps[len(early):]:
         li.step(s)
-    gp_rows.forward()
+    for s in steps[1:]:
+        at_step(s, multiply_back)
     for k in order:
         first_copy(k).wait_send()
-    gp_rows.end()
-    fetch_gp = pltpu.make_async_copy(gp_panel, part, load_sem.at[2])
-    fetch_gp.start()
-    load_wi.wait()
-    fetch_gp.wait()
-
-    @pl.loop(0, part.shape[0] // TALL)
-    def _(i):
-        r = pl.ds(pl.multiple_of(i * TALL, TALL), TALL)
-
-        @pl.loop(0, wi.shape[0] // COLS)
-        def _(j):
-            k = pl.ds(pl.multiple_of(j * COLS, COLS), COLS)
-            product[r, k] = width_contract(part[r, :], wi[k, :]).astype(BF16)
+    gp_rows.wait_sends()
 
     store = pltpu.make_async_copy(product, out_panel, load_sem.at[2])
     store.start()
@@ -422,6 +458,7 @@
             pltpu.VMEM((d, f), BF16),
             pltpu.VMEM((f, d), BF16),
             pltpu.VMEM((2 * t, d), BF16),
+            pltpu.VMEM((2 * t, f), BF16),
             pltpu.VMEM((tokens, f), BF16),
             pltpu.VMEM((tokens, d), BF16),
             pltpu.VMEM((rows, f), BF16),

time: 265 us -> 267 us (level); the launches traced: 264 us -> 262 us
  waiting for transfers between devices: 23.5 us -> 19.2 us
  Pallas kernels: 158 us -> 161 us
    pallas_call x1, Pallas kernels: 158 us -> 161 us  [hidden(): pl.pallas_call(functools.partial(hidden_kernel, n_row, n_col), out_shape=...]
  transfers between devices with their start and end apart: 10 -> 10, of which waited for: 4 -> 3; matrix products, arithmetic and copies ran while one was open for 17% -> 17% of each run, Pallas kernels for 0% -> 0%
where the time goes in v4:
time: 267 us; the launch traced here: 262 us
  Pallas kernels  161 us (60%)
  matrix products  38.1 us (14%)
  waiting for transfers between devices  19.2 us (7%)
  starting transfers between devices  18.6 us (7%)
  other arithmetic  9.69 us (4%)
  between operations  8.77 us (3%)
  local copies, waits for them, and re-layouts  6.48 us (2%)
    pallas_call x1, Pallas kernels, hidden(): pl.pallas_call(functools.partial(hidden_kernel, n_row, n_col), out_shape=...  161 us
    dot_general x2, matrix products, token_contract(): lax.dot_general(left, right, (((0,), (0,)), ((), ())), preferred_element_...  38.1 us
    ppermute x3, starting transfers between devices, col_scatter(): up = lax.ppermute(going_up.astype(BF16), 'col', ups)  11 us
    ppermute x3, waiting for transfers between devices, col_scatter(): down = lax.ppermute(going_down.astype(BF16), 'col', downs)  8.98 us
    ppermute x4, waiting for transfers between devices, col_scatter(): got = lax.ppermute(away, 'col', swap)  8.98 us
  transfers between devices with their start and end apart: 10, of which 3 were waited for; matrix products, arithmetic and copies ran while one was open for 17% of the time, Pallas kernels for 0%

profile of v4, /device:TPU:0, one launch (start us, length us, event | category | flops | bytes accessed | tf_op | source)
XLA Modules:
  0.0 262.1 jit_solution(13705974414839784018)
XLA Ops:
  0.7 1.6 constant_dynamic-slice_fusion.8
  4.8 161.3 %hidden.1 = (bf16[1024,3072]{1,0:T(8,128)(2,1)}, bf16[1024,3072]{1,0:T(8,128)(2,1)}, bf16[1024,2048]{1,0:T(8,128)(2,1)}, bf16[1024,2048]{1,0:T(8,128)(2,1)}, bf16[1024,3072]{1,0:T(8,128)(2,1)}) custom-call(bf16[128,3072]{1,0:T(8,128)(2,1)} %li_ref.1, bf16[128,3072]{1,0:T(8,128)(2,1)} %og_ref.1, bf16[256,2048]{1,0:T(8,128)(2,1)} %pre_ref.1, ...), custom_call_target="tpu_custom_call" | custom-call | flops 25769803776 | bytes 67108864 | tf_op jit(solution)/shard_map/hidden/pallas_call | solution.py:446
  166.1 4.0 %constant_dynamic-slice_fusion.6 = (bf16[128,3072]{1,0:T(8,128)(2,1)}, bf16[128,3072]{1,0:T(8,128)(2,1)S(1)}, bf16[128,3072]{1,0:T(8,128)(2,1)S(1)}, bf16[128,30...) fusion(bf16[1024,3072]{1,0:T(8,128)(2,1)} %get-tuple-element.12, s32[]{:T(128)S(6)} %select_n.112, ...), kind=kLoop, calls=%fused_computation.16 | loop fusion | bytes 9437208 | tf_op jit(solution)/shard_map/dynamic_slice | solution.py:507
  170.1 0.5 collective-permute-start.3
  170.7 1.5 collective-permute-start.2
  172.2 19.2 %fusion.3 = f32[2048,3072]{1,0:T(8,128)} fusion(bf16[1024,2048]{1,0:T(8,128)(2,1)} %get-tuple-element.16, bf16[1024,3072]{1,0:T(8,128)(2,1)S(1)} %copy-done.1), kind=kOutput, calls=%fused_computation.22 | convolution fusion | flops 12884901888 | bytes 35651584 | tf_op jit(solution)/shard_map/dot_general | solution.py:27
  191.3 0.2 add_convert_fusion.5
  191.5 2.2 collective-permute-start.4
  193.7 1.6 collective-permute-start.7
  195.3 0.6 collective-permute-start.1
  195.8 1.5 collective-permute-start
  198.5 9.0 %collective-permute-done.2 = bf16[128,3072]{1,0:T(8,128)(2,1)S(1)} collective-permute-done((bf16[128,3072]{1,0:T(8,128)(2,1)}, bf16[128,3072]{1,0:T(8,128)(2,1)S(1)}, u32[]{:S(2)}, u32[]{:S(2)}) %collective-permute-start.2) | collective-permute-done | bytes 786464 | tf_op jit(solution)/shard_map/ppermute | solution.py:511
  207.5 0.9 copy-done
  208.3 2.3 add_convert_fusion.4
  210.6 3.3 %collective-permute-start.5 = (bf16[128,3072]{1,0:T(8,128)(2,1)S(1)}, bf16[128,3072]{1,0:T(8,128)(2,1)S(1)}, u32[]{:S(2)}, u32[]{:S(2)}) collective-permute-start(bf16[128,3072]{1,0:T(8,128)(2,1)S(1)} %get-tuple-element.21), channel_id=1, source_target_pairs={{0,2},{1,3},{2,4},{3,5},{8,10},{9,11},{10,12},{11,13},{16,18},{17,... | collective-permute-start | bytes 2359304 | tf_op jit(solution)/shard_map/ppermute | solution.py:520
  214.0 1.5 add_convert_fusion.2
  215.5 0.7 collective-permute-start.8
  216.2 19.0 %fusion.2 = f32[3072,2048]{1,0:T(8,128)} fusion(bf16[1024,3072]{1,0:T(8,128)(2,1)S(1)} %copy-done.2, bf16[1024,2048]{1,0:T(8,128)(2,1)} %get-tuple-element.14), kind=kOutput, calls=%fused_computation.21 | convolution fusion | flops 12884901888 | bytes 35651584 | tf_op jit(solution)/shard_map/dot_general | solution.py:27
  237.6 2.0 add_convert_fusion.3
  239.5 1.3 collective-permute-start.9
  240.8 5.5 %collective-permute-start.6 = (bf16[128,3072]{1,0:T(8,128)(2,1)}, bf16[128,3072]{1,0:T(8,128)(2,1)}, u32[]{:S(2)}, u32[]{:S(2)}) collective-permute-start(bf16[128,3072]{1,0:T(8,128)(2,1)} %get-tuple-element.29), channel_id=1, source_target_pairs={{0,2},{1,3},{2,4},{3,5},{4,6},{5,7},{8,10},{9,11},{10,12},{11,13},... | collective-permute-start | bytes 2359304 | tf_op jit(solution)/shard_map/ppermute | solution.py:520
  248.2 9.0 %collective-permute-done.9 = bf16[128,3072]{1,0:T(8,128)(2,1)} collective-permute-done((bf16[128,3072]{1,0:T(8,128)(2,1)}, bf16[128,3072]{1,0:T(8,128)(2,1)}, u32[]{:S(2)}, u32[]{:S(2)}) %collective-permute-start.9) | collective-permute-done | bytes 786464 | tf_op jit(solution)/shard_map/ppermute | solution.py:521
  257.2 1.2 collective-permute-done.6
  258.4 3.7 %add_convert_fusion = bf16[128,3072]{1,0:T(8,128)(2,1)} fusion(bf16[128,3072]{1,0:T(8,128)(2,1)} %collective-permute-done.9, bf16[128,3072]{1,0:T(8,128)(2,1)} %collective-permute-done.6, bf16[128,3072]{1,0:T(8,128)(2,1)} %collective-permute-done, bf16[128,3072]{1,0:T(8,128)(2,1)S(1)} %get-tuple-element.22, bf16[128,3072]{1,0:T(8,128)(2,1)S(1)} %add_convert_fusion.5, ...), kind=kLoop, calls=%fused_computation | loop fusion | flops 6684672 | bytes 7077895 | tf_op jit(solution)/shard_map/convert_element_type | solution.py:522
  (12 shorter events, 0.0 us)
Async XLA Ops:
  166.1 6.1 %copy-start.1 = (bf16[1024,3072]{1,0:T(8,128)(2,1)S(1)}, bf16[1024,3072]{1,0:T(8,128)(2,1)}, u32[]{:S(2)}) copy-start(bf16[1024,3072]{1,0:T(8,128)(2,1)} %get-tuple-element.17) | copy-start | bytes 18874372
  170.1 21.2 %collective-permute-start.3 = (bf16[128,3072]{1,0:T(8,128)(2,1)S(1)}, bf16[128,3072]{1,0:T(8,128)(2,1)S(1)}, u32[]{:S(2)}, u32[]{:S(2)}) collective-permute-start(bf16[128,3072]{1,0:T(8,128)(2,1)S(1)} %get-tuple-element.24), channel_id=1, source_target_pairs={{0,1},{1,0},{2,3},{3,2},{4,5},{5,4},{6,7},{7,6},{8,9},{9,8},{10,11... | collective-permute-start | bytes 2359304 | tf_op jit(solution)/shard_map/ppermute | solution.py:511
  170.7 36.8 %collective-permute-start.2 = (bf16[128,3072]{1,0:T(8,128)(2,1)}, bf16[128,3072]{1,0:T(8,128)(2,1)S(1)}, u32[]{:S(2)}, u32[]{:S(2)}) collective-permute-start(bf16[128,3072]{1,0:T(8,128)(2,1)} %get-tuple-element.26), channel_id=1, source_target_pairs={{0,1},{1,0},{2,3},{3,2},{4,5},{5,4},{6,7},{7,6},{8,9},{9,8},{10,11... | collective-permute-start | bytes 2359304 | tf_op jit(solution)/shard_map/ppermute | solution.py:511
  191.5 16.0 %collective-permute-start.4 = (bf16[128,3072]{1,0:T(8,128)(2,1)S(1)}, bf16[128,3072]{1,0:T(8,128)(2,1)}, u32[]{:S(2)}, u32[]{:S(2)}) collective-permute-start(bf16[128,3072]{1,0:T(8,128)(2,1)S(1)} %add_convert_fusion.5), channel_id=1, source_target_pairs={{0,2},{1,3},{8,10},{9,11},{16,18},{17,19},{24,26},{25,27}} | collective-permute-start | bytes 2359304 | tf_op jit(solution)/shard_map/ppermute | solution.py:520
  193.7 20.3 %collective-permute-start.7 = (bf16[128,3072]{1,0:T(8,128)(2,1)S(1)}, bf16[128,3072]{1,0:T(8,128)(2,1)}, u32[]{:S(2)}, u32[]{:S(2)}) collective-permute-start(bf16[128,3072]{1,0:T(8,128)(2,1)S(1)} %add_convert_fusion.5), channel_id=1, source_target_pairs={{7,5},{6,4},{15,13},{14,12},{23,21},{22,20},{31,29},{30,28}} | collective-permute-start | bytes 2359304 | tf_op jit(solution)/shard_map/ppermute | solution.py:521
  195.3 42.3 %collective-permute-start.1 = (bf16[128,3072]{1,0:T(8,128)(2,1)}, bf16[128,3072]{1,0:T(8,128)(2,1)S(1)}, u32[]{:S(2)}, u32[]{:S(2)}) collective-permute-start(bf16[128,3072]{1,0:T(8,128)(2,1)} %get-tuple-element.27), channel_id=1, source_target_pairs={{0,1},{1,0},{2,3},{3,2},{4,5},{5,4},{6,7},{7,6},{8,9},{9,8},{10,11... | collective-permute-start | bytes 2359304 | tf_op jit(solution)/shard_map/ppermute | solution.py:511
  195.8 52.4 %collective-permute-start = (bf16[128,3072]{1,0:T(8,128)(2,1)}, bf16[128,3072]{1,0:T(8,128)(2,1)}, u32[]{:S(2)}, u32[]{:S(2)}) collective-permute-start(bf16[128,3072]{1,0:T(8,128)(2,1)} %get-tuple-element.23), channel_id=1, source_target_pairs={{0,1},{1,0},{2,3},{3,2},{4,5},{5,4},{6,7},{7,6},{8,9},{9,8},{10,11... | collective-permute-start | bytes 2359304 | tf_op jit(solution)/shard_map/ppermute | solution.py:511
  207.5 0.9 copy-start
  208.3 7.9 %copy-start.2 = (bf16[1024,3072]{1,0:T(8,128)(2,1)S(1)}, bf16[1024,3072]{1,0:T(8,128)(2,1)}, u32[]{:S(2)}) copy-start(bf16[1024,3072]{1,0:T(8,128)(2,1)} %get-tuple-element.13) | copy-start | bytes 18874372
  210.6 26.9 %collective-permute-start.5 = (bf16[128,3072]{1,0:T(8,128)(2,1)S(1)}, bf16[128,3072]{1,0:T(8,128)(2,1)S(1)}, u32[]{:S(2)}, u32[]{:S(2)}) collective-permute-start(bf16[128,3072]{1,0:T(8,128)(2,1)S(1)} %get-tuple-element.21), channel_id=1, source_target_pairs={{0,2},{1,3},{2,4},{3,5},{8,10},{9,11},{10,12},{11,13},{16,18},{17,... | collective-permute-start | bytes 2359304 | tf_op jit(solution)/shard_map/ppermute | solution.py:520
  215.5 22.1 %collective-permute-start.8 = (bf16[128,3072]{1,0:T(8,128)(2,1)S(1)}, bf16[128,3072]{1,0:T(8,128)(2,1)S(1)}, u32[]{:S(2)}, u32[]{:S(2)}) collective-permute-start(bf16[128,3072]{1,0:T(8,128)(2,1)S(1)} %add_convert_fusion.2), channel_id=1, source_target_pairs={{7,5},{6,4},{5,3},{4,2},{15,13},{14,12},{13,11},{12,10},{23,21},{2... | collective-permute-start | bytes 2359304 | tf_op jit(solution)/shard_map/ppermute | solution.py:521
  239.5 17.7 %collective-permute-start.9 = (bf16[128,3072]{1,0:T(8,128)(2,1)}, bf16[128,3072]{1,0:T(8,128)(2,1)}, u32[]{:S(2)}, u32[]{:S(2)}) collective-permute-start(bf16[128,3072]{1,0:T(8,128)(2,1)} %get-tuple-element.30), channel_id=1, source_target_pairs={{7,5},{6,4},{5,3},{4,2},{3,1},{2,0},{15,13},{14,12},{13,11},{12,10... | collective-permute-start | bytes 2359304 | tf_op jit(solution)/shard_map/ppermute | solution.py:521
  240.8 17.6 %collective-permute-start.6 = (bf16[128,3072]{1,0:T(8,128)(2,1)}, bf16[128,3072]{1,0:T(8,128)(2,1)}, u32[]{:S(2)}, u32[]{:S(2)}) collective-permute-start(bf16[128,3072]{1,0:T(8,128)(2,1)} %get-tuple-element.29), channel_id=1, source_target_pairs={{0,2},{1,3},{2,4},{3,5},{4,6},{5,7},{8,10},{9,11},{10,12},{11,13},... | collective-permute-start | bytes 2359304 | tf_op jit(solution)/shard_map/ppermute | solution.py:520
